TPU v7x, 512 devices: a whole 4x4x16 slice. The times are simulated.
512 devices in a mesh: prompt: 8 (over x, z_hi), trainer: 16 (over z_lo, core), tensor: 4 (over y).
Axes of the slice: x: 4, y: 4, z: 16 (z_hi: 2, z_lo: 8; z = z_hi * 8 + z_lo), core: 2. Of those that a mesh axis runs over, the one named last changes fastest.
Arguments:
- queries: bfloat16 [8, 16, 256, 2560], P('prompt', 'trainer', None, 'tensor'), may hold values from -72 to 72
- resp_keys: bfloat16 [8, 16, 256, 512], P('prompt', 'trainer', None, 'tensor'), may hold values from -72 to 72
- resp_values: bfloat16 [8, 16, 256, 512], P('prompt', 'trainer', None, 'tensor'), may hold values from -6 to 6
- prompt_keys: bfloat16 [8, 512, 512], P('prompt', 'trainer', 'tensor'), may hold values from -6 to 6
- prompt_values: bfloat16 [8, 512, 512], P('prompt', 'trainer', 'tensor'), may hold values from -6 to 6
- q_gain: float32 [2560], P('tensor'), may hold values from 1 to 3
- k_gain: float32 [512], P('tensor'), may hold values from 1 to 3
- lengths: int32 [8, 16], P('prompt', 'trainer'), may hold values from 1 to 256, 2048 in all within a row
- block_rank: int32 [8, 16, 2], P('prompt'), may hold values from 0 to 15, as said below
- out_grad: bfloat16 [8, 16, 256, 2560], P('prompt', 'trainer', None, 'tensor'), may hold values from -6 to 6
Outputs:
- attn_out: bfloat16 [8, 16, 256, 2560], P('prompt', 'trainer', None, 'tensor')
- grad_queries: bfloat16 [8, 16, 256, 2560], P('prompt', 'trainer', None, 'tensor')
- grad_keys: bfloat16 [8, 16, 256, 512], P('prompt', 'trainer', None, 'tensor')
- grad_values: bfloat16 [8, 16, 256, 512], P('prompt', 'trainer', None, 'tensor')
- grad_prompt_keys: bfloat16 [8, 512, 512], P('prompt', 'trainer', 'tensor')
- grad_prompt_values: bfloat16 [8, 512, 512], P('prompt', 'trainer', 'tensor')
- grad_q_gain: float32 [2560], P('tensor')
- grad_k_gain: float32 [512], P('tensor')
Inputs may be any that keep to these rules, and one draw needn't show every extreme that they name: In each group the 16 response lengths sum to 2048, and the longest is 256. Block b of the response at trainer index t of group g goes to slot b of rank block_rank[g, t, b]. For each g and b the ranks over t are a permutation of the 16 ranks, and the 2 blocks of one response go to different ranks.
All inputs are finite; a program needn't handle non-finite values.
Results may differ from a plain program's by a relative error of at most 0.018.
The roundings to bfloat16 on the way count: a program that leaves them out, or rounds other values in their place, can miss the bound.
Values may be sent and summed in bfloat16 or wider, within the bound.
No kernel may reach another device: no remote copies, remote signals or barrier semaphores. Data moves between devices by JAX's collectives and lax.ppermute only.
A program may use at most 64 MiB of HBM per device.

v0:
```python
import jax
import jax.numpy as jnp
from jax import lax
from jax.sharding import PartitionSpec as P

HEAD = 128
HEADS = 20
KV_HEADS = 4
BLOCK = 128
BLOCKS = 2


epsilon = 1e-06


def contract_last(left, right):
    return lax.dot_general(
        left, right, (((1,), (1,)), ((), ())), preferred_element_type=jnp.float32
    )


def contract_first(left, right):
    return lax.dot_general(
        left, right, (((0,), (0,)), ((), ())), preferred_element_type=jnp.float32
    )


def select_blocks(selector, blocks):
    picked = lax.dot_general(
        selector, blocks, (((1,), (0,)), ((), ())), preferred_element_type=jnp.float32
    )
    return picked.astype(jnp.bfloat16)


def masked_scores(query_head, key_list, length, prompt_count, query_start):
    row_count = query_head.shape[0]
    score_scale = query_head.shape[1] ** (-0.5)
    raw_scores = contract_last(query_head, key_list) * score_scale
    query_pos = jnp.arange(row_count, dtype=jnp.int32)[:, None] + query_start
    key_pos = jnp.arange(key_list.shape[0], dtype=jnp.int32)[None, :] - prompt_count
    allowed = (key_pos < 0) | (key_pos <= query_pos) & (key_pos < length)
    return jnp.where(allowed, raw_scores, -1e30)


def forward_head(query_head, key_list, value_list, length, prompt_count, query_start):
    scores = masked_scores(query_head, key_list, length, prompt_count, query_start)
    row_max = jnp.max(scores, axis=1, keepdims=True)
    log_total = row_max + jnp.log(jnp.sum(jnp.exp(scores - row_max), axis=1, keepdims=True))
    weights = jnp.exp(scores - log_total).astype(jnp.bfloat16)
    return (jnp.dot(weights, value_list, preferred_element_type=jnp.float32), log_total)


def backward_head(
    query_head,
    key_list,
    value_list,
    grad_head,
    out_head,
    log_total,
    length,
    prompt_count,
    query_start,
):
    score_scale = query_head.shape[1] ** (-0.5)
    scores = masked_scores(query_head, key_list, length, prompt_count, query_start)
    weights = jnp.exp(scores - log_total)
    row_inner = jnp.sum(
        grad_head.astype(jnp.float32) * out_head.astype(jnp.float32), axis=1, keepdims=True
    )
    prob_grad = contract_last(grad_head, value_list)
    score_grad = (weights * (prob_grad - row_inner) * score_scale).astype(jnp.bfloat16)
    grad_query = jnp.dot(score_grad, key_list, preferred_element_type=jnp.float32)
    grad_keylist = contract_first(score_grad, query_head)
    grad_valuelist = contract_first(weights.astype(jnp.bfloat16), grad_head)
    return (grad_query, grad_keylist, grad_valuelist)


def build_lists(prompt_key_all, prompt_value_all, key_rows, value_rows):
    key_lists = [jnp.concatenate([prompt_key_all, key_rows], axis=0)]
    value_lists = [jnp.concatenate([prompt_value_all, value_rows], axis=0)]
    return (key_lists, value_lists)


def attend_forward(
    query_n,
    key_lists,
    value_lists,
    live_rows,
    length,
    prompt_count,
    group_size,
    head_size,
    query_start,
):
    pieces = []
    totals = []
    for member in range(group_size):
        query_head = query_n[:, member * head_size : (member + 1) * head_size]
        attended, log_total = forward_head(
            query_head, key_lists[0], value_lists[0], length, prompt_count, query_start
        )
        pieces.append(attended)
        totals.append(log_total)
    home_out = (jnp.concatenate(pieces, axis=1) * live_rows[:, None]).astype(jnp.bfloat16)
    return (home_out, totals)


def attend_backward(
    query_n,
    key_lists,
    value_lists,
    grad_live,
    out_rows,
    totals,
    length,
    prompt_count,
    group_size,
    head_size,
    query_start,
):
    query_parts = []
    key_total = jnp.zeros((key_lists[0].shape[0], head_size), jnp.float32)
    value_total = jnp.zeros((key_lists[0].shape[0], head_size), jnp.float32)
    for member in range(group_size):
        first = member * head_size
        grad_query, grad_keylist, grad_valuelist = backward_head(
            query_n[:, first : first + head_size],
            key_lists[0],
            value_lists[0],
            grad_live[:, first : first + head_size],
            out_rows[:, first : first + head_size],
            totals[member],
            length,
            prompt_count,
            query_start,
        )
        query_parts.append(grad_query)
        key_total = key_total + grad_keylist
        value_total = value_total + grad_valuelist
    return (jnp.concatenate(query_parts, axis=1), key_total, value_total)


def on_device(
    queries,
    resp_keys,
    resp_values,
    prompt_keys,
    prompt_values,
    q_gain,
    k_gain,
    lengths,
    block_rank,
    out_grad,
):
    head_size = HEAD
    group_size = HEADS // KV_HEADS
    row_count = queries.shape[2]
    query_width = queries.shape[3]
    key_width = resp_keys.shape[3]
    raw_query = queries[0, 0].astype(jnp.float32)
    raw_key = resp_keys[0, 0].astype(jnp.float32)
    query_sums, key_sums = lax.psum(
        (jnp.sum(raw_query * raw_query, axis=1), jnp.sum(raw_key * raw_key, axis=1)), "tensor"
    )
    query_factor = lax.rsqrt(query_sums / (HEADS * HEAD) + epsilon)[:, None]
    key_factor = lax.rsqrt(key_sums / (KV_HEADS * HEAD) + epsilon)[:, None]
    normed_query = raw_query * query_factor
    normed_key = raw_key * key_factor
    query_n = (normed_query * q_gain).astype(jnp.bfloat16)
    key_n = (normed_key * k_gain).astype(jnp.bfloat16)
    prompt_key_all, prompt_value_all = (
        lax.all_gather(prompt_keys[0], "trainer", axis=0, tiled=True),
        lax.all_gather(prompt_values[0], "trainer", axis=0, tiled=True),
    )
    prompt_count = prompt_key_all.shape[0]
    value_n = resp_values[0, 0]
    own_rank = lax.axis_index("trainer")
    rank_table = block_rank[0]
    rank_ids = jnp.arange(rank_table.shape[0], dtype=jnp.int32)
    own_targets = lax.dynamic_index_in_dim(rank_table, own_rank, 0, keepdims=False)
    arrivals = (rank_table == own_rank).astype(jnp.bfloat16)
    slot_sources = (jnp.transpose(rank_table) == own_rank).astype(jnp.bfloat16)
    destinations = (own_targets[:, None] == rank_ids[None, :]).astype(jnp.bfloat16)
    rank_slots = (rank_ids[:, None] == own_targets[None, :]).astype(jnp.bfloat16)
    grad_blocks = out_grad[0, 0].reshape(BLOCKS, BLOCK, query_width)
    length = lengths[0, 0]
    live_rows = (jnp.arange(row_count, dtype=jnp.int32) < length).astype(jnp.float32)
    key_lists, value_lists = build_lists(prompt_key_all, prompt_value_all, key_n, value_n)
    home_out, totals = attend_forward(
        query_n, key_lists, value_lists, live_rows, length, prompt_count, group_size, head_size, 0
    )
    out_blocks = home_out.reshape(BLOCKS, BLOCK, query_width)
    sent_out, came_back = (
        lax.all_to_all(
            select_blocks(rank_slots, out_blocks),
            "trainer",
            split_axis=0,
            concat_axis=0,
            tiled=True,
        ),
        lax.all_to_all(
            select_blocks(arrivals, grad_blocks), "trainer", split_axis=0, concat_axis=0, tiled=True
        ),
    )
    attn_blocks = select_blocks(slot_sources, sent_out)
    grad_home = select_blocks(destinations, came_back).reshape(row_count, query_width)
    grad_live = grad_home * live_rows.astype(jnp.bfloat16)[:, None]
    grad_qn, key_terms, value_terms = attend_backward(
        query_n,
        key_lists,
        value_lists,
        grad_live,
        home_out,
        totals,
        length,
        prompt_count,
        group_size,
        head_size,
        0,
    )
    grad_kn = key_terms[prompt_count:]
    grad_values = value_terms[prompt_count:].astype(jnp.bfloat16)
    prompt_terms = jnp.concatenate([key_terms[:prompt_count], value_terms[:prompt_count]], axis=1)
    reduced = lax.psum_scatter(
        prompt_terms.astype(jnp.bfloat16), "trainer", scatter_dimension=0, tiled=True
    ).astype(jnp.float32)
    grad_prompt_keys = reduced[:, :key_width].astype(jnp.bfloat16)
    grad_prompt_values = reduced[:, key_width:].astype(jnp.bfloat16)
    query_inner = grad_qn * q_gain
    key_inner = grad_kn * k_gain
    query_mix, key_mix = lax.psum(
        (jnp.sum(query_inner * normed_query, axis=1), jnp.sum(key_inner * normed_key, axis=1)),
        "tensor",
    )
    grad_queries = (
        query_factor * (query_inner - normed_query * (query_mix / (HEADS * HEAD))[:, None])
    ).astype(jnp.bfloat16)
    grad_keys = (
        key_factor * (key_inner - normed_key * (key_mix / (KV_HEADS * HEAD))[:, None])
    ).astype(jnp.bfloat16)
    gain_query, gain_key = lax.psum(
        (jnp.sum(grad_qn * normed_query, axis=0), jnp.sum(grad_kn * normed_key, axis=0)),
        ("prompt", "trainer"),
    )
    return (
        attn_blocks.reshape(1, 1, row_count, query_width),
        grad_queries[None, None],
        grad_keys[None, None],
        grad_values[None, None],
        grad_prompt_keys[None],
        grad_prompt_values[None],
        gain_query,
        gain_key,
    )


def solution(mesh):
    placed = (
        P("prompt", "trainer", None, "tensor"),
        P("prompt", "trainer", None, "tensor"),
        P("prompt", "trainer", None, "tensor"),
        P("prompt", "trainer", "tensor"),
        P("prompt", "trainer", "tensor"),
        P("tensor"),
        P("tensor"),
        P("prompt", "trainer"),
        P("prompt", None, None),
        P("prompt", "trainer", None, "tensor"),
    )
    return jax.shard_map(
        on_device,
        mesh=mesh,
        in_specs=placed,
        out_specs=(
            P("prompt", "trainer", None, "tensor"),
            P("prompt", "trainer", None, "tensor"),
            P("prompt", "trainer", None, "tensor"),
            P("prompt", "trainer", None, "tensor"),
            P("prompt", "trainer", "tensor"),
            P("prompt", "trainer", "tensor"),
            P("tensor"),
            P("tensor"),
        ),
        check_vma=False,
    )
```

profile of v0, /device:TPU:1, one launch (start us, length us, event | category | flops | bytes accessed | tf_op | source)
XLA Modules:
  0.0 581.8 jit_solution(574363196858729128)
XLA Ops:
  7.2 1.0 copy-done
  8.1 1.9 convolution_convert_fusion
  10.0 2.1 copy.70
  12.2 14.2 %all-to-all-start.1 = ((bf16[16,128,640]{2,1,0:T(8,128)(2,1)}), bf16[16,128,640]{2,1,0:T(8,128)(2,1)}, u32[]{:S(2)}, u32[]{:S(2)}) async-start(bf16[16,128,640]{2,1,0:T(8,128)(2,1)} %copy.70), calls=%async_computation.1 | async-start | bytes 5242880 | tf_op jit(solution)/shard_map/all_to_all | solution.py:201
  28.3 9.5 %all-reduce.2 = (f32[256]{0:T(256)S(1)}, f32[256]{0:T(256)S(1)}) all-reduce(f32[256]{0:T(256)S(1)} %fusion.46, f32[256]{0:T(256)S(1)} %fusion.63), channel_id=1, replica_groups=mesh['prompt'=8,'trainer'=16,'tensor'=4] {'tensor'}, use_global_device_ids=true, to_apply=%region_1.0 | all-reduce | flops 512 | bytes 4096 | tf_op jit(solution)/shard_map/psum | solution.py:162
  38.1 93.9 %all-gather = bf16[1,512,128]{2,1,0:T(8,128)(2,1)S(1)} all-gather(bf16[1,32,128]{2,1,0:T(8,128)(2,1)S(1)} %copy-done.30), channel_id=2, replica_groups=mesh['prompt'=8,'trainer'=16,'tensor'=4] {'trainer'}, dimensions={1}, use_global_device_ids=true | all-gather | bytes 139264 | tf_op jit(solution)/shard_map/all_gather | solution.py:172
  132.0 50.6 %all-gather.1 = bf16[1,512,128]{2,1,0:T(8,128)(2,1)S(1)} all-gather(bf16[1,32,128]{2,1,0:T(8,128)(2,1)S(1)} %copy-done.31), channel_id=3, replica_groups=mesh['prompt'=8,'trainer'=16,'tensor'=4] {'trainer'}, dimensions={1}, use_global_device_ids=true | all-gather | bytes 139264 | tf_op jit(solution)/shard_map/all_gather | solution.py:173
  189.2 0.8 copy-done.14
  190.2 1.7 convolution_convert_fusion.1
  191.8 2.1 copy.66
  193.9 4.5 all-to-all-start
  198.7 1.3 multiply_convert_fusion
  200.0 3.4 fusion.27
  209.6 0.8 copy.78
  210.4 1.3 bitcast_dynamic-update-slice_fusion.4
  213.0 0.8 copy-done.13
  214.4 9.5 %all-reduce.1 = (f32[256]{0:T(256)S(1)}, f32[256]{0:T(256)S(1)}) all-reduce(f32[256]{0:T(256)S(1)} %get-tuple-element.41, f32[256]{0:T(256)S(1)} %get-tuple-element.48), channel_id=1, replica_groups=mesh['prompt'=8,'trainer'=16,'tensor'=4] {'tensor'}, use_global_device_ids=true, to_apply=%region_20.21 | all-reduce | flops 512 | bytes 4096 | tf_op jit(solution)/shard_map/psum | solution.py:231
  223.9 1.2 fusion.50
  225.2 74.6 %all-to-all-done = bf16[16,128,640]{2,1,0:T(8,128)(2,1)} async-done(((bf16[16,128,640]{2,1,0:T(8,128)(2,1)}), bf16[16,128,640]{2,1,0:T(8,128)(2,1)}, u32[]{:S(2)}, u32[]{:S(2)}) %all-to-all-start) | async-done | bytes 2621472 | tf_op jit(solution)/shard_map/all_to_all | solution.py:194
  299.7 3.4 fusion.24
  303.1 0.8 copy.68
  304.6 0.9 copy.73
  305.6 0.7 copy.74
  306.3 266.3 %all-reduce = (f32[640]{0:T(1024)}, f32[128]{0:T(128)}) all-reduce(f32[640]{0:T(1024)S(1)} %get-tuple-element.40, f32[128]{0:T(128)S(1)} %get-tuple-element.47), channel_id=1, replica_groups=mesh['prompt'=8,'trainer'=16,'tensor'=4] {'prompt','trainer'}, use_global_device_ids=true, to_apply=%region_25.26 | all-reduce | flops 768 | bytes 6144 | tf_op jit(solution)/shard_map/psum | solution.py:241
  (157 shorter events, 18.9 us)
Async XLA Ops:
  12.2 14.9 %copy-start.28 = (s32[1,16,2]{1,2,0:T(2,128)S(1)}, s32[1,16,2]{1,2,0:T(2,128)}, u32[]{:S(2)}) copy-start(s32[1,16,2]{1,2,0:T(2,128)} %param.18) | copy-start | bytes 388
  12.2 15.7 %copy-start.18 = (bf16[1,1,256,128]{3,2,1,0:T(8,128)(2,1)S(1)}, bf16[1,1,256,128]{3,2,1,0:T(8,128)(2,1)}, u32[]{:S(2)}) copy-start(bf16[1,1,256,128]{3,2,1,0:T(8,128)(2,1)} %param.11) | copy-start | bytes 196612
  12.2 15.8 %copy-start.17 = (bf16[1,1,256,640]{3,2,1,0:T(8,128)(2,1)S(1)}, bf16[1,1,256,640]{3,2,1,0:T(8,128)(2,1)}, u32[]{:S(2)}) copy-start(bf16[1,1,256,640]{3,2,1,0:T(8,128)(2,1)} %param.10) | copy-start | bytes 983044
  12.2 25.7 %copy-start.32 = (f32[128]{0:T(128)S(1)}, f32[128]{0:T(128)}, u32[]{:S(2)}) copy-start(f32[128]{0:T(128)} %param.16) | copy-start | bytes 1540
  12.2 25.9 %copy-start.30 = (bf16[1,32,128]{2,1,0:T(8,128)(2,1)S(1)}, bf16[1,32,128]{2,1,0:T(8,128)(2,1)}, u32[]{:S(2)}) copy-start(bf16[1,32,128]{2,1,0:T(8,128)(2,1)} %param.13) | copy-start | bytes 24580
  12.2 119.8 %copy-start.31 = (bf16[1,32,128]{2,1,0:T(8,128)(2,1)S(1)}, bf16[1,32,128]{2,1,0:T(8,128)(2,1)}, u32[]{:S(2)}) copy-start(bf16[1,32,128]{2,1,0:T(8,128)(2,1)} %param.14) | copy-start | bytes 24580
  12.2 170.5 %copy-start.19 = (f32[640]{0:T(1024)S(1)}, f32[640]{0:T(1024)}, u32[]{:S(2)}) copy-start(f32[640]{0:T(1024)} %param.15) | copy-start | bytes 7684
  12.2 181.7 %all-to-all-start.1 = ((bf16[16,128,640]{2,1,0:T(8,128)(2,1)}), bf16[16,128,640]{2,1,0:T(8,128)(2,1)}, u32[]{:S(2)}, u32[]{:S(2)}) async-start(bf16[16,128,640]{2,1,0:T(8,128)(2,1)} %copy.70), calls=%async_computation.1 | async-start | bytes 5242880 | tf_op jit(solution)/shard_map/all_to_all | solution.py:201
  182.8 2.9 copy-start.11
  186.5 2.1 copy-start.20
  186.5 2.1 copy-start.22
  187.5 2.7 copy-start.34
  193.9 6.0 %copy-start.35 = (s32[2]{0:T(128)S(1)}, s32[2]{0:T(128)}, u32[]{:S(2)}) copy-start(s32[2]{0:T(128)} %dynamic-slice_reduce_fusion) | copy-start | bytes 28
  193.9 105.8 %all-to-all-start = ((bf16[16,128,640]{2,1,0:T(8,128)(2,1)}), bf16[16,128,640]{2,1,0:T(8,128)(2,1)}, u32[]{:S(2)}, u32[]{:S(2)}) async-start(bf16[16,128,640]{2,1,0:T(8,128)(2,1)} %copy.66), calls=%async_computation | async-start | bytes 5242880 | tf_op jit(solution)/shard_map/all_to_all | solution.py:194
  198.4 374.2 %reduce-scatter.4.cloned.1.call-start = ((), (), s32[]{:S(2)}) async-start(), calls=%async_computation.3 | async-start | bytes 278528
  198.7 4.9 copy-start.4
  198.7 4.9 copy-start.27
  200.0 4.0 copy-start.2
  200.0 4.0 copy-start.25
  209.0 2.8 copy-start.9
  209.5 2.6 copy-start.7
  210.4 3.5 copy-start.33
  212.4 87.3 %copy-start.29 = (s32[1,16,2]{1,2,0:T(2,128)S(1)}, s32[1,16,2]{1,2,0:T(2,128)}, u32[]{:S(2)}) copy-start(s32[1,16,2]{1,2,0:T(2,128)} %param.18) | copy-start | bytes 388
  214.1 89.0 %copy-start.16 = (bf16[768,128]{0,1:T(8,128)(2,1)S(1)}, bf16[768,128]{0,1:T(8,128)(2,1)}, u32[]{:S(2)}) copy-start(bf16[768,128]{0,1:T(8,128)(2,1)} %copy-done.15) | copy-start | bytes 589828
  (16 other events, 21.6 us)
Sparse Core Ops, SparseCore 0:
  210.6 117.2 reduce-scatter.3
where the time goes:
time: 586 us; the launch traced here: 582 us
  blocking collectives  430 us (73%)
  waiting for transfers between devices  74.6 us (13%)
  matrix products  21.3 us (4%)
  starting transfers between devices  18.9 us (3%)
  local copies, waits for them, and re-layouts  16.3 us (3%)
  between operations  15.6 us (3%)
    psum x1, blocking collectives, on_device(): lax.psum((jnp.sum(grad_qn * normed_query, axis=0), jnp.sum(grad_kn * norm...  266 us
    all_gather x1, blocking collectives, on_device(): lax.all_gather(prompt_keys[0], 'trainer', axis=0, tiled=True)  93.9 us
    all_to_all x1, waiting for transfers between devices, on_device(): lax.all_to_all(select_blocks(rank_slots, out_blocks), 'trainer', split_ax...  74.6 us
    all_gather x1, blocking collectives, on_device(): lax.all_gather(prompt_values[0], 'trainer', axis=0, tiled=True)  50.6 us
    all_to_all x1, starting transfers between devices, on_device(): lax.all_to_all(select_blocks(arrivals, grad_blocks), 'trainer', split_axi...  14.2 us
  transfers between devices with their start and end apart: 3, of which 1 were waited for; matrix products, arithmetic and copies ran while one was open for 6% of the time, Pallas kernels for 0%

commit v1 on v0

v1 whole, which is shorter than its diff:
```python
import jax
import jax.numpy as jnp
from jax import lax
from jax.experimental import pallas as pl
from jax.experimental.pallas import tpu as pltpu
from jax.sharding import PartitionSpec as P

HEAD = 128
HEADS = 20
KV_HEADS = 4
GROUP = HEADS // KV_HEADS
BLOCK = 128
BLOCKS = 2
RESP = BLOCK * BLOCKS
PROMPT = 512
KEYS = PROMPT + RESP
CHUNKS = KEYS // BLOCK
PROMPT_CHUNKS = PROMPT // BLOCK
N_TRAINER = 16
N_TENSOR = 4
PROMPTS = ("x", "zhi")
TRAINER = ("zlo", "core")
WIDTH = GROUP * HEAD
GAIN_ROWS = (GROUP + 1) // 2
SCALE = HEAD ** (-0.5)

epsilon = 1e-06
f32 = jnp.float32
bf16 = jnp.bfloat16

PARAMS = pltpu.CompilerParams(vmem_limit_bytes=24 * 1024 * 1024)
VMEM = pl.BlockSpec(memory_space=pltpu.VMEM)
SMEM = pl.BlockSpec(memory_space=pltpu.SMEM)


def nt(left, right):
    return lax.dot_general(left, right, (((1,), (1,)), ((), ())), preferred_element_type=f32)


def nn(left, right):
    return jnp.dot(left, right, preferred_element_type=f32)


def columns_to_tile(columns):
    wide = [jnp.broadcast_to(c, (BLOCK, BLOCK)).T[:1] for c in columns]
    wide.append(jnp.zeros((8 - len(columns), BLOCK), f32))
    return jnp.concatenate(wide, axis=0)


def tile_to_columns(tile):
    turned = jnp.concatenate([tile] * (BLOCK // 8), axis=0).T
    first = jnp.concatenate([turned[:, 0:1], turned[:, 1:2]], axis=0)
    second = jnp.concatenate([turned[:, 2:3], turned[:, 3:4]], axis=0)
    return first, second


def factors(sums_ref):
    total = sums_ref[0]
    for i in range(1, N_TENSOR):
        total = total + sums_ref[i]
    query_sums, key_sums = tile_to_columns(total)
    query_factor = lax.rsqrt(query_sums / (HEADS * HEAD) + epsilon)
    key_factor = lax.rsqrt(key_sums / (KV_HEADS * HEAD) + epsilon)
    return query_factor, key_factor


def stats_kernel(q_ref, k_ref, pk_ref, pv_ref, sums_ref, kv_ref):
    raw_query = q_ref[...].astype(f32)
    raw_key = k_ref[...].astype(f32)
    query_sums = jnp.sum(raw_query * raw_query, axis=1, keepdims=True)
    key_sums = jnp.sum(raw_key * raw_key, axis=1, keepdims=True)
    tile = columns_to_tile(
        [query_sums[:BLOCK], query_sums[BLOCK:], key_sums[:BLOCK], key_sums[BLOCK:]]
    )
    for i in range(N_TENSOR):
        sums_ref[i] = tile
    pair = jnp.concatenate([pk_ref[...], pv_ref[...]], axis=1)
    for i in range(N_TRAINER):
        kv_ref[i] = pair


def masked(scores, chunk, length):
    if chunk < PROMPT_CHUNKS:
        return scores
    key_pos = lax.broadcasted_iota(jnp.int32, scores.shape, 0) + (chunk - PROMPT_CHUNKS) * BLOCK
    query_pos = lax.broadcasted_iota(jnp.int32, scores.shape, 1)
    return jnp.where((key_pos <= query_pos) & (key_pos < length), scores, -1e30)


def live_column(length):
    rows = lax.broadcasted_iota(jnp.int32, (RESP, 1), 0)
    return (rows < length).astype(f32)


def forward_kernel(
    info_ref, q_ref, k_ref, v_ref, kv_ref, sums_ref, qg_ref, kg_ref,
    qn_ref, keys_ref, lse_ref, out_ref,
    values_t_ref, s_ref, p_ref,
):
    length = info_ref[0]
    query_factor, key_factor = factors(sums_ref)
    qn_ref[...] = (q_ref[...].astype(f32) * query_factor * qg_ref[...]).astype(bf16)
    keys_ref[:PROMPT] = kv_ref[:, :HEAD]
    keys_ref[PROMPT:] = (k_ref[...].astype(f32) * key_factor * kg_ref[...]).astype(bf16)
    values_t_ref[:, :PROMPT] = kv_ref[:, HEAD:].astype(f32).T.astype(bf16)
    values_t_ref[:, PROMPT:] = v_ref[...].astype(f32).T.astype(bf16)
    live = live_column(length)
    for h in range(GROUP):
        cols = slice(h * HEAD, (h + 1) * HEAD)
        query = qn_ref[:, cols]
        top = None
        for c in range(CHUNKS):
            rows = slice(c * BLOCK, (c + 1) * BLOCK)
            scores = masked(nt(keys_ref[rows], query) * SCALE, c, length)
            s_ref[rows] = scores
            most = jnp.max(scores, axis=0, keepdims=True)
            top = most if top is None else jnp.maximum(top, most)
        total = jnp.zeros_like(top)
        for c in range(CHUNKS):
            rows = slice(c * BLOCK, (c + 1) * BLOCK)
            grown = jnp.exp(s_ref[rows] - top)
            s_ref[rows] = grown
            total = total + jnp.sum(grown, axis=0, keepdims=True)
        share = 1.0 / total
        for c in range(CHUNKS):
            rows = slice(c * BLOCK, (c + 1) * BLOCK)
            p_ref[rows] = (s_ref[rows] * share).astype(bf16)
        lse_ref[h : h + 1] = top + jnp.log(total)
        attended = nn(values_t_ref[...], p_ref[...]).T
        out_ref[:, cols] = (attended * live).astype(bf16)
    lse_ref[GROUP:] = jnp.zeros((8 - GROUP, RESP), f32)


def backward_kernel(
    info_ref, q_ref, k_ref, v_ref, kv_ref, sums_ref, qg_ref, kg_ref,
    qn_ref, keys_ref, lse_ref, out_ref, own_ref, passed_ref,
    u_ref, w_ref, gv_ref, terms_ref, mix_ref, gain_ref,
    keys_t_ref, grad_ref, ds_ref, dk_ref, dv_ref,
):
    length = info_ref[0]
    query_factor, key_factor = factors(sums_ref)
    keys_t_ref[...] = keys_ref[...].astype(f32).T.astype(bf16)
    live = live_column(length).astype(bf16)
    swapped = info_ref[1] != 0
    first = jnp.where(swapped, passed_ref[...], own_ref[...])
    second = jnp.where(swapped, own_ref[...], passed_ref[...])
    grad_ref[:BLOCK] = first * live[:BLOCK]
    grad_ref[BLOCK:] = second * live[BLOCK:]
    query_mix = jnp.zeros((RESP, 1), f32)
    gain_rows = []
    for h in range(GROUP):
        cols = slice(h * HEAD, (h + 1) * HEAD)
        query = qn_ref[:, cols]
        grad = grad_ref[:, cols]
        inner = (grad.astype(f32) * out_ref[:, cols].astype(f32)).T
        inner = jnp.sum(inner, axis=0, keepdims=True)
        lse = lse_ref[h : h + 1]
        for c in range(CHUNKS):
            rows = slice(c * BLOCK, (c + 1) * BLOCK)
            if c < PROMPT_CHUNKS:
                value = kv_ref[rows, HEAD:]
            else:
                value = v_ref[(c - PROMPT_CHUNKS) * BLOCK : (c - PROMPT_CHUNKS + 1) * BLOCK]
            scores = masked(nt(keys_ref[rows], query) * SCALE, c, length)
            weights = jnp.exp(scores - lse)
            prob_grad = nt(value, grad)
            score_grad = (weights * (prob_grad - inner) * SCALE).astype(bf16)
            ds_ref[rows] = score_grad
            key_term = nn(score_grad, query)
            value_term = nn(weights.astype(bf16), grad)
            if h == 0:
                dk_ref[rows] = key_term
                dv_ref[rows] = value_term
            else:
                dk_ref[rows] += key_term
                dv_ref[rows] += value_term
        grad_qn = nn(keys_t_ref[...], ds_ref[...]).T
        normed = q_ref[:, cols].astype(f32) * query_factor
        u = grad_qn * qg_ref[:, cols]
        u_ref[:, cols] = u
        query_mix = query_mix + jnp.sum(u * normed, axis=1, keepdims=True)
        gain_rows.append(jnp.sum(grad_qn * normed, axis=0, keepdims=True))
    terms_ref[:, :HEAD] = dk_ref[:PROMPT]
    terms_ref[:, HEAD:] = dv_ref[:PROMPT]
    gv_ref[...] = dv_ref[PROMPT:].astype(bf16)
    grad_kn = dk_ref[PROMPT:]
    normed_key = k_ref[...].astype(f32) * key_factor
    w = grad_kn * kg_ref[...]
    w_ref[...] = w
    key_mix = jnp.sum(w * normed_key, axis=1, keepdims=True)
    gain_rows.append(jnp.sum(grad_kn * normed_key, axis=0, keepdims=True))
    gains = jnp.concatenate(
        [jnp.concatenate(gain_rows[i : i + 2], axis=1) for i in range(0, GROUP + 1, 2)], axis=0
    )
    gain_ref[...] = jnp.concatenate(
        [gains, jnp.zeros((8 - GAIN_ROWS, 2 * HEAD), f32)], axis=0
    )
    tile = columns_to_tile([query_mix[:BLOCK], query_mix[BLOCK:], key_mix[:BLOCK], key_mix[BLOCK:]])
    mix_ref[...] = tile


def final_kernel(q_ref, k_ref, sums_ref, u_ref, w_ref, *refs):
    *mix_refs, gq_ref, gk_ref = refs
    query_factor, key_factor = factors(sums_ref)
    total = mix_refs[0][...]
    for mix_ref in mix_refs[1:]:
        total = total + mix_ref[...]
    query_mix, key_mix = tile_to_columns(total)
    normed = q_ref[...].astype(f32) * query_factor
    gq_ref[...] = (
        query_factor * (u_ref[...] - normed * (query_mix / (HEADS * HEAD)))
    ).astype(bf16)
    normed_key = k_ref[...].astype(f32) * key_factor
    gk_ref[...] = (
        key_factor * (w_ref[...] - normed_key * (key_mix / (KV_HEADS * HEAD)))
    ).astype(bf16)


def call(kernel, outs, specs, scratch, flops, *args):
    return pl.pallas_call(
        kernel,
        out_shape=[jax.ShapeDtypeStruct(s, d) for s, d in outs],
        in_specs=specs,
        out_specs=[VMEM] * len(outs),
        scratch_shapes=[pltpu.VMEM(s, d) for s, d in scratch],
        compiler_params=PARAMS,
        cost_estimate=pl.CostEstimate(flops=flops, bytes_accessed=0, transcendentals=0),
    )(*args)


def after(array, *others):
    return lax.optimization_barrier((array,) + others)[0]


def swap(array, even, odd):
    pairs = [(i, i ^ (odd if i % 2 else even)) for i in range(N_TRAINER)]
    return lax.ppermute(array, TRAINER, pairs)


class Route:
    def __init__(self, me, source):
        self.me, self.source = me, source
        self.core = me & 1
        self.first = jnp.where(self.core == 0, 8, 4)
        self.last = 12 - self.first

    def pair(self, blocks):
        mine = lax.dynamic_index_in_dim(blocks, self.core, 0, keepdims=False)
        other = lax.dynamic_index_in_dim(blocks, 1 - self.core, 0, keepdims=False)
        return jnp.stack([mine, swap(other, 1, 1)])

    def four(self, pair, *earlier):
        return jnp.concatenate([pair, after(swap(pair, 8, 4), *earlier)], axis=0)

    def eight(self, four):
        return four, swap(four, 2, 2)

    def pick(self, eight, source):
        offset = source ^ self.me
        slot = bit(offset, 1) + 2 * bit(offset, self.first)
        near, far = (lax.dynamic_index_in_dim(four, slot, 0, keepdims=False) for four in eight)
        return jnp.where((offset & 2) != 0, far, near)

    def wanted(self, eight):
        there = self.me ^ self.last
        return jnp.stack([self.pick(eight, self.source(there ^ i, self.core)) for i in range(2)])

    def found(self, eight, wanted, *earlier):
        came = after(swap(wanted, 4, 8), *earlier)
        found = []
        for i in range(2):
            source = self.source(self.me ^ i, self.core)
            far = ((source ^ self.me) & self.last) != 0
            found.append(jnp.where(far, came[i], self.pick(eight, source)))
        return found

    def passed(self, found):
        return swap(found, 1, 1)


def bit(number, mask):
    return jnp.where((number & mask) != 0, 1, 0)


def on_device(
    queries,
    resp_keys,
    resp_values,
    prompt_keys,
    prompt_values,
    q_gain,
    k_gain,
    lengths,
    block_rank,
    out_grad,
):
    me = lax.axis_index(TRAINER)
    core = me & 1
    table = block_rank[0]
    ranks = jnp.arange(N_TRAINER, dtype=jnp.int32)

    def home_source(dest, b):
        return lax.dynamic_index_in_dim(table[:, b], dest, 0, keepdims=False)

    def balanced_source(dest, b):
        return jnp.sum(jnp.where(table[:, b] == dest, ranks, 0))

    query, key, value = queries[0, 0], resp_keys[0, 0], resp_values[0, 0]
    q_row, k_row = q_gain[None], k_gain[None]

    sums, pairs = call(
        stats_kernel,
        [((N_TENSOR, 8, BLOCK), f32), ((N_TRAINER, PROMPT // N_TRAINER, 2 * HEAD), bf16)],
        [VMEM] * 4,
        [],
        0,
        query,
        key,
        prompt_keys[0],
        prompt_values[0],
    )
    to_home = Route(me, home_source)
    grad_pair, sums, pairs = lax.optimization_barrier(
        (to_home.pair(out_grad.reshape(BLOCKS, BLOCK, WIDTH)), sums, pairs)
    )
    sums = lax.all_to_all(sums, "tensor", 0, 0, tiled=True)
    grad_four = to_home.four(grad_pair, sums)
    grad_four, pairs = lax.optimization_barrier((grad_four, pairs))
    grad_eight = to_home.eight(grad_four)
    pairs = lax.all_to_all(pairs, TRAINER, 0, 0, tiled=True).reshape(PROMPT, 2 * HEAD)
    grad_wanted = to_home.wanted(grad_eight)
    pairs = after(pairs, grad_wanted)
    grad_found = to_home.found(grad_eight, grad_wanted)
    info = jnp.stack([lengths[0, 0], core])
    shared = (query, key, value, pairs, sums, q_row, k_row)
    query_n, key_list, lse, home_out = call(
        forward_kernel,
        [((RESP, WIDTH), bf16), ((KEYS, HEAD), bf16), ((8, RESP), f32), ((RESP, WIDTH), bf16)],
        [SMEM] + [VMEM] * 7,
        [((HEAD, KEYS), bf16), ((KEYS, RESP), f32), ((KEYS, RESP), bf16)],
        0,
        info,
        *shared,
    )

    to_ranks = Route(me, balanced_source)
    out_pair = to_ranks.pair(home_out.reshape(BLOCKS, BLOCK, WIDTH))
    grad_found[1], out_pair = lax.optimization_barrier((grad_found[1], out_pair))
    out_four = to_ranks.four(out_pair)
    grad_own = grad_found[0]
    grad_passed = to_home.passed(grad_found[1])

    u, w, grad_values, terms, mix, gains = call(
        backward_kernel,
        [
            ((RESP, WIDTH), f32),
            ((RESP, HEAD), f32),
            ((RESP, HEAD), bf16),
            ((PROMPT, 2 * HEAD), f32),
            ((8, BLOCK), f32),
            ((8, 2 * HEAD), f32),
        ],
        [SMEM] + [VMEM] * 13,
        [
            ((HEAD, KEYS), bf16),
            ((RESP, WIDTH), bf16),
            ((KEYS, RESP), bf16),
            ((KEYS, HEAD), f32),
            ((KEYS, HEAD), f32),
        ],
        0,
        info,
        *shared,
        query_n,
        key_list,
        lse,
        home_out,
        grad_own,
        grad_passed,
    )
    out_four, gains, terms = lax.optimization_barrier((out_four, gains, terms))
    out_eight = to_ranks.eight(out_four)
    turns = [[(i, (i + k) % N_TENSOR) for i in range(N_TENSOR)] for k in range(1, N_TENSOR)]
    mix = [mix] + [lax.ppermute(mix, "tensor", turn) for turn in turns]
    owned = PROMPT // N_TRAINER
    terms = jnp.concatenate(
        [
            terms.reshape(N_TRAINER, owned, 2 * HEAD),
            jnp.broadcast_to(gains[None], (N_TRAINER,) + gains.shape),
        ],
        axis=1,
    ).reshape(N_TRAINER // 2, 2, owned + gains.shape[0], 2 * HEAD)
    near, far = (
        lax.dynamic_index_in_dim(terms, i, 1, keepdims=False) for i in (core, 1 - core)
    )
    terms = (near + swap(far.astype(bf16), 1, 1).astype(f32)).astype(bf16)
    terms = lax.all_to_all(terms, "zlo", 0, 0, tiled=True)
    terms = jnp.sum(terms.astype(f32), axis=0)
    gains = terms[owned : owned + GAIN_ROWS]
    terms = terms[:owned].astype(bf16)
    out_wanted = to_ranks.wanted(out_eight)
    gains = after(gains, out_wanted)
    gains = lax.all_to_all(
        jnp.broadcast_to(gains[None], (lax.axis_size(PROMPTS),) + gains.shape),
        PROMPTS,
        0,
        0,
        tiled=True,
    )
    gains = jnp.sum(gains, axis=0).reshape(-1)
    out_found = to_ranks.found(out_eight, out_wanted)

    out_own, out_passed = out_found[0], to_ranks.passed(after(out_found[1], gains))
    attn_out = jnp.where(
        core == 0,
        jnp.concatenate([out_own, out_passed], axis=0),
        jnp.concatenate([out_passed, out_own], axis=0),
    )
    grad_queries, grad_keys = call(
        final_kernel,
        [((RESP, WIDTH), bf16), ((RESP, HEAD), bf16)],
        [VMEM] * (5 + N_TENSOR),
        [],
        0,
        query,
        key,
        sums,
        u,
        w,
        *mix,
    )
    return (
        attn_out[None, None],
        grad_queries[None, None],
        grad_keys[None, None],
        grad_values[None, None],
        terms[None, :, :HEAD],
        terms[None, :, HEAD:],
        gains[:WIDTH],
        gains[WIDTH : WIDTH + HEAD],
    )


def solution(mesh):
    n_zhi = 2 if mesh.shape["prompt"] % 2 == 0 else 1
    shape = (mesh.shape["prompt"] // n_zhi, n_zhi, N_TRAINER // 2, 2, N_TENSOR)
    fine = jax.sharding.Mesh(mesh.devices.reshape(shape), PROMPTS + TRAINER + ("tensor",))
    rows = P(PROMPTS, TRAINER, None, "tensor")
    tokens = P(PROMPTS, TRAINER, "tensor")
    return jax.shard_map(
        on_device,
        mesh=fine,
        in_specs=(
            rows,
            rows,
            rows,
            tokens,
            tokens,
            P("tensor"),
            P("tensor"),
            P(PROMPTS, TRAINER),
            P(PROMPTS, None, None),
            rows,
        ),
        out_specs=(rows, rows, rows, rows, tokens, tokens, P("tensor"), P("tensor")),
        check_vma=False,
    )
```

time: 586 us -> 167 us (0.28)
  blocking collectives: 430 us -> 6.56 us
  starting transfers between devices: 18.9 us -> 110 us
  waiting for transfers between devices: 74.6 us -> 22.8 us
  matrix products: 21.3 us -> 0 us
  Pallas kernels: 0 us -> 12.6 us
  local copies, waits for them, and re-layouts: 16.3 us -> 4.84 us
  between operations: 15.6 us -> 6.97 us
    psum x3 -> x0, blocking collectives: 285 us -> none  [the longest x1 266 us: on_device(): lax.psum((jnp.sum(grad_qn * normed_query, axis=0), jnp.sum(grad_kn * norm...]
    all_gather x2 -> x0, blocking collectives: 145 us -> none  [the longest x1 93.9 us: on_device(): lax.all_gather(prompt_keys[0], 'trainer', axis=0, tiled=True)]
    ppermute x0 -> x14, starting transfers between devices: none -> 71.7 us  [the longest x11 62.2 us: swap(): return lax.ppermute(array, TRAINER, pairs)]
    all_to_all x2 -> x3, waiting for transfers between devices: 74.6 us -> 11.9 us  [the longest x1 10.3 us: on_device(): lax.all_to_all(pairs, TRAINER, 0, 0, tiled=True).reshape(PROMPT, 2 * HEAD)]
    dot_general x34 -> x0, matrix products: 21.3 us -> none  [the longest x4 10.3 us: select_blocks(): lax.dot_general(selector, blocks, (((1,), (0,)), ((), ())), preferred_ele...]
    all_to_all x2 -> x3, starting transfers between devices: 18.7 us -> 37.9 us  [the longest x1 17.1 us: on_device(): lax.all_to_all(pairs, TRAINER, 0, 0, tiled=True).reshape(PROMPT, 2 * HEAD)]
    pallas_call x0 -> x4, Pallas kernels: none -> 12.6 us  [call(): pl.pallas_call(kernel, out_shape=[jax.ShapeDtypeStruct(s, d) for s, d in...]
    ppermute x0 -> x14, waiting for transfers between devices: none -> 10.9 us  [the longest x11 9.26 us: swap(): return lax.ppermute(array, TRAINER, pairs)]
  transfers between devices with their start and end apart: 3 -> 17, of which waited for: 1 -> 10; matrix products, arithmetic and copies ran while one was open for 6% -> 3% of each run, Pallas kernels for 0% -> 8%
where the time goes in v1:
time: 167 us; the launch traced here: 166 us
  starting transfers between devices  110 us (66%)
  waiting for transfers between devices  22.8 us (14%)
  Pallas kernels  12.6 us (8%)
  between operations  6.97 us (4%)
  blocking collectives  6.56 us (4%)
  local copies, waits for them, and re-layouts  4.84 us (3%)
  other arithmetic  2.88 us (2%)
    ppermute x11, starting transfers between devices, swap(): return lax.ppermute(array, TRAINER, pairs)  62.2 us
    all_to_all x1, starting transfers between devices, on_device(): lax.all_to_all(pairs, TRAINER, 0, 0, tiled=True).reshape(PROMPT, 2 * HEAD)  17.1 us
    all_to_all x1, starting transfers between devices, on_device(): lax.all_to_all(jnp.broadcast_to(gains[None], (lax.axis_size(PROMPTS),) +...  16.9 us
    pallas_call x4, Pallas kernels, call(): pl.pallas_call(kernel, out_shape=[jax.ShapeDtypeStruct(s, d) for s, d in...  12.6 us
    all_to_all x1, waiting for transfers between devices, on_device(): lax.all_to_all(pairs, TRAINER, 0, 0, tiled=True).reshape(PROMPT, 2 * HEAD)  10.3 us
    ppermute x3, starting transfers between devices, on_device(): mix = [mix] + [lax.ppermute(mix, 'tensor', turn) for turn in turns]  9.48 us
    ppermute x11, waiting for transfers between devices, swap(): return lax.ppermute(array, TRAINER, pairs)  9.26 us
    all_to_all x1, blocking collectives, on_device(): sums = lax.all_to_all(sums, 'tensor', 0, 0, tiled=True)  6.56 us
  transfers between devices with their start and end apart: 17, of which 10 were waited for; matrix products, arithmetic and copies ran while one was open for 3% of the time, Pallas kernels for 8%

profile of v1, /device:TPU:1, one launch (start us, length us, event | category | flops | bytes accessed | tf_op | source)
XLA Modules:
  0.0 166.3 jit_solution(9620336958538964216)
XLA Ops:
  1.8 8.8 %collective-permute-start = (bf16[128,640]{1,0:T(8,128)(2,1)S(1)}, bf16[128,640]{1,0:T(8,128)(2,1)S(1)}, u32[]{:S(2)}, u32[]{:S(2)}) collective-permute-start(bf16[128,640]{1,0:T(8,128)(2,1)S(1)} %get-tuple-element.79), channel_id=1, source_target_pairs={{0,4},{4,0},{8,12},{12,8},{16,20},{20,16},{24,28},{28,24},{32,36},... | collective-permute-start | bytes 491528 | tf_op jit(solution)/shard_map/ppermute | solution.py:237
  11.6 1.9 %collective-permute-start.1 = (bf16[2,128,640]{2,1,0:T(8,128)(2,1)S(1)}, bf16[2,128,640]{2,1,0:T(8,128)(2,1)S(1)}, u32[]{:S(2)}, u32[]{:S(2)}) collective-permute-start(bf16[2,128,640]{2,1,0:T(8,128)(2,1)S(1)} %pad_maximum_fusion.2), channel_id=1, source_target_pairs={{0,32},{4,20},{8,40},{12,28},{16,48},{20,4},{24,56},{28,12},{32,0}... | collective-permute-start | bytes 983048 | tf_op jit(solution)/shard_map/ppermute | solution.py:237
  13.5 6.6 %all_to_all.20.sums_ref = f32[4,8,128]{2,1,0:T(8,128)S(1)} all-to-all(f32[4,8,128]{2,1,0:T(8,128)S(1)} %get-tuple-element.39), channel_id=1, replica_groups=mesh['x'=4,'zhi'=2,'zlo'=8,'core'=2,'tensor'=4] {'tensor'}, dimensions={0} | all-to-all | bytes 32768 | tf_op jit(solution)/shard_map/all_to_all | solution.py:326
  20.1 3.2 %collective-permute-done.1 = bf16[2,128,640]{2,1,0:T(8,128)(2,1)S(1)} collective-permute-done((bf16[2,128,640]{2,1,0:T(8,128)(2,1)S(1)}, bf16[2,128,640]{2,1,0:T(8,128)(2,1)S(1)}, u32[]{:S(2)}, u32[]{:S(2)}) %collective-permute-start.1) | collective-permute-done | bytes 327712 | tf_op jit(solution)/shard_map/ppermute | solution.py:237
  23.4 3.9 %collective-permute-start.2 = (bf16[4,128,640]{2,1,0:T(8,128)(2,1)S(1)}, bf16[4,128,640]{2,1,0:T(8,128)(2,1)S(1)}, u32[]{:S(2)}, u32[]{:S(2)}) collective-permute-start(bf16[4,128,640]{2,1,0:T(8,128)(2,1)S(1)} %pad_maximum_fusion), channel_id=1, source_target_pairs={{0,8},{4,12},{8,0},{12,4},{16,24},{20,28},{24,16},{28,20},{32,40},... | collective-permute-start | bytes 1966088 | tf_op jit(solution)/shard_map/ppermute | solution.py:237
  27.3 17.1 %all-to-all-start.1 = ((bf16[16,32,256]{2,1,0:T(8,128)(2,1)}), bf16[16,32,256]{2,1,0:T(8,128)(2,1)S(1)}, u32[]{:S(2)}, u32[]{:S(2)}) async-start(bf16[16,32,256]{2,1,0:T(8,128)(2,1)} %get-tuple-element.43), calls=%async_computation.1 | async-start | bytes 524288 | tf_op jit(solution)/shard_map/all_to_all | solution.py:330
  47.2 7.3 %collective-permute-start.3 = (bf16[2,128,640]{2,1,0:T(8,128)(2,1)S(1)}, bf16[2,128,640]{2,1,0:T(8,128)(2,1)S(1)}, u32[]{:S(2)}, u32[]{:S(2)}) collective-permute-start(bf16[2,128,640]{2,1,0:T(8,128)(2,1)S(1)} %pad_maximum_fusion.3), channel_id=1, source_target_pairs={{0,16},{4,36},{8,24},{12,44},{16,0},{20,52},{24,8},{28,60},{32,48}... | collective-permute-start | bytes 983048 | tf_op jit(solution)/shard_map/ppermute | solution.py:237
  56.6 10.3 %all-to-all-done.1 = bf16[16,32,256]{2,1,0:T(8,128)(2,1)S(1)} async-done(((bf16[16,32,256]{2,1,0:T(8,128)(2,1)}), bf16[16,32,256]{2,1,0:T(8,128)(2,1)S(1)}, u32[]{:S(2)}, u32[]{:S(2)}) %all-to-all-start.1) | async-done | bytes 262176 | tf_op jit(solution)/shard_map/all_to_all | solution.py:330
  67.5 3.5 %shard_map.162 = (bf16[256,640]{1,0:T(8,128)(2,1)S(1)}, bf16[768,128]{1,0:T(8,128)(2,1)S(1)}, f32[8,256]{1,0:T(8,128)S(1)}, bf16[256,640]{1,0:T(8,128)(2,1)S(1)}) custom-call(s32[2]{0:T(128)S(1)} %pad_add_fusion.info_ref, bf16[256,640]{1,0:T(8,128)(2,1)S(1)} %bitcast.65, bf16[256,128]{1,0:T(8,128)(2,1)S(1)} %bitcast.74, bf16[256,128]{1,0:T(8,128)(2,1)S(1)} %bitcast.77, ...), custom_call_target="tpu_custom_call" | custom-call | tf_op jit(solution)/shard_map/pallas_call | solution.py:220
  71.1 1.9 %collective-permute-start.4 = (bf16[128,640]{1,0:T(8,128)(2,1)S(1)}, bf16[128,640]{1,0:T(8,128)(2,1)S(1)}, u32[]{:S(2)}, u32[]{:S(2)}) collective-permute-start(bf16[128,640]{1,0:T(8,128)(2,1)S(1)} %get-tuple-element.77), channel_id=1, source_target_pairs={{0,4},{4,0},{8,12},{12,8},{16,20},{20,16},{24,28},{28,24},{32,36},... | collective-permute-start | bytes 491528 | tf_op jit(solution)/shard_map/ppermute | solution.py:237
  73.0 2.0 %collective-permute-done.3 = bf16[2,128,640]{2,1,0:T(8,128)(2,1)S(1)} collective-permute-done((bf16[2,128,640]{2,1,0:T(8,128)(2,1)S(1)}, bf16[2,128,640]{2,1,0:T(8,128)(2,1)S(1)}, u32[]{:S(2)}, u32[]{:S(2)}) %collective-permute-start.3) | collective-permute-done | bytes 327712 | tf_op jit(solution)/shard_map/ppermute | solution.py:237
  75.1 2.7 %collective-permute-start.5 = (bf16[2,128,640]{2,1,0:T(8,128)(2,1)S(1)}, bf16[2,128,640]{2,1,0:T(8,128)(2,1)S(1)}, u32[]{:S(2)}, u32[]{:S(2)}) collective-permute-start(bf16[2,128,640]{2,1,0:T(8,128)(2,1)S(1)} %pad_maximum_fusion.4), channel_id=1, source_target_pairs={{0,32},{4,20},{8,40},{12,28},{16,48},{20,4},{24,56},{28,12},{32,0}... | collective-permute-start | bytes 983048 | tf_op jit(solution)/shard_map/ppermute | solution.py:237
  77.8 3.0 %collective-permute-start.6 = (bf16[128,640]{1,0:T(8,128)(2,1)S(1)}, bf16[128,640]{1,0:T(8,128)(2,1)S(1)}, u32[]{:S(2)}, u32[]{:S(2)}) collective-permute-start(bf16[128,640]{1,0:T(8,128)(2,1)S(1)} %get-tuple-element.50), channel_id=1, source_target_pairs={{0,4},{4,0},{8,12},{12,8},{16,20},{20,16},{24,28},{28,24},{32,36},... | collective-permute-start | bytes 491528 | tf_op jit(solution)/shard_map/ppermute | solution.py:237
  81.8 7.2 %shard_map.163 = (f32[256,640]{1,0:T(8,128)S(1)}, f32[256,128]{1,0:T(8,128)S(1)}, bf16[256,128]{1,0:T(8,128)(2,1)}, f32[512,256]{1,0:T(8,128)S(1)}, f32[8,128]{1,0:T(8,128)S(1)}, /*index=5*/f32[8,256]{1,0:T(8,128)S(1)}) custom-call(s32[2]{0:T(128)S(1)} %pad_add_fusion.info_ref, bf16[256,640]{1,0:T(8,128)(2,1)S(1)} %bitcast.66, ...), custom_call_target="tpu_custom_call" | custom-call | tf_op jit(solution)/shard_map/pallas_call | solution.py:220
  89.0 1.9 %collective-permute-done.5 = bf16[2,128,640]{2,1,0:T(8,128)(2,1)S(1)} collective-permute-done((bf16[2,128,640]{2,1,0:T(8,128)(2,1)S(1)}, bf16[2,128,640]{2,1,0:T(8,128)(2,1)S(1)}, u32[]{:S(2)}, u32[]{:S(2)}) %collective-permute-start.5) | collective-permute-done | bytes 327712 | tf_op jit(solution)/shard_map/ppermute | solution.py:237
  91.0 4.5 %collective-permute-start.7 = (bf16[4,128,640]{2,1,0:T(8,128)(2,1)S(1)}, bf16[4,128,640]{2,1,0:T(8,128)(2,1)S(1)}, u32[]{:S(2)}, u32[]{:S(2)}) collective-permute-start(bf16[4,128,640]{2,1,0:T(8,128)(2,1)S(1)} %pad_maximum_fusion.1), channel_id=1, source_target_pairs={{0,8},{4,12},{8,0},{12,4},{16,24},{20,28},{24,16},{28,20},{32,40},... | collective-permute-start | bytes 1966088 | tf_op jit(solution)/shard_map/ppermute | solution.py:237
  95.6 6.5 %collective-permute-start.9 = (bf16[8,40,256]{2,1,0:T(8,128)(2,1)S(1)}, bf16[8,40,256]{2,1,0:T(8,128)(2,1)S(1)}, u32[]{:S(2)}, u32[]{:S(2)}) collective-permute-start(bf16[8,40,256]{2,1,0:T(8,128)(2,1)S(1)} %fusion.6), channel_id=1, source_target_pairs={{0,4},{4,0},{8,12},{12,8},{16,20},{20,16},{24,28},{28,24},{32,36},... | collective-permute-start | bytes 491528 | tf_op jit(solution)/shard_map/ppermute | solution.py:237
  103.8 3.9 %all-to-all-start.2 = ((bf16[8,40,256]{2,1,0:T(8,128)(2,1)}), bf16[8,40,256]{2,1,0:T(8,128)(2,1)S(1)}, u32[]{:S(2)}, u32[]{:S(2)}) async-start(bf16[8,40,256]{2,1,0:T(8,128)(2,1)} %fusion.5), calls=%async_computation.2 | async-start | bytes 327680 | tf_op jit(solution)/shard_map/all_to_all | solution.py:397
  109.7 7.3 %collective-permute-start.8 = (bf16[2,128,640]{2,1,0:T(8,128)(2,1)S(1)}, bf16[2,128,640]{2,1,0:T(8,128)(2,1)S(1)}, u32[]{:S(2)}, u32[]{:S(2)}) collective-permute-start(bf16[2,128,640]{2,1,0:T(8,128)(2,1)S(1)} %pad_maximum_fusion.5), channel_id=1, source_target_pairs={{0,16},{4,36},{8,24},{12,44},{16,0},{20,52},{24,8},{28,60},{32,48}... | collective-permute-start | bytes 983048 | tf_op jit(solution)/shard_map/ppermute | solution.py:237
  119.0 16.9 %all-to-all-start.3 = ((f32[8,3,256]{2,1,0:T(4,128)}), f32[8,3,256]{2,1,0:T(4,128)S(1)}, u32[]{:S(2)}, u32[]{:S(2)}) async-start(f32[8,3,256]{2,1,0:T(4,128)} %broadcast_in_dim.45), calls=%async_computation.3 | async-start | bytes 65536 | tf_op jit(solution)/shard_map/all_to_all | solution.py:403
  136.0 4.6 %collective-permute-start.13 = (f32[8,128]{1,0:T(8,128)S(1)}, f32[8,128]{1,0:T(8,128)S(1)}, u32[]{:S(2)}, u32[]{:S(2)}) collective-permute-start(f32[8,128]{1,0:T(8,128)S(1)} %get-tuple-element.60.refs_0_), channel_id=1, source_target_pairs={{0,3},{1,0},{2,1},{3,2},{4,7},{5,4},{6,5},{7,6},{8,11},{9,8},{10,9... | collective-permute-start | bytes 12296 | tf_op jit(solution)/shard_map/ppermute | solution.py:384
  140.6 2.3 %collective-permute-start.12 = (f32[8,128]{1,0:T(8,128)S(1)}, f32[8,128]{1,0:T(8,128)S(1)}, u32[]{:S(2)}, u32[]{:S(2)}) collective-permute-start(f32[8,128]{1,0:T(8,128)S(1)} %get-tuple-element.60.refs_0_), channel_id=1, source_target_pairs={{0,2},{1,3},{2,0},{3,1},{4,6},{5,7},{6,4},{7,5},{8,10},{9,11},{10,... | collective-permute-start | bytes 12296 | tf_op jit(solution)/shard_map/ppermute | solution.py:384
  142.9 2.6 %collective-permute-start.11 = (f32[8,128]{1,0:T(8,128)S(1)}, f32[8,128]{1,0:T(8,128)S(1)}, u32[]{:S(2)}, u32[]{:S(2)}) collective-permute-start(f32[8,128]{1,0:T(8,128)S(1)} %get-tuple-element.60.refs_0_), channel_id=1, source_target_pairs={{0,1},{1,2},{2,3},{3,0},{4,5},{5,6},{6,7},{7,4},{8,9},{9,10},{10,1... | collective-permute-start | bytes 12296 | tf_op jit(solution)/shard_map/ppermute | solution.py:384
  149.9 14.4 %collective-permute-start.10 = (bf16[128,640]{1,0:T(8,128)(2,1)S(1)}, bf16[128,640]{1,0:T(8,128)(2,1)S(1)}, u32[]{:S(2)}, u32[]{:S(2)}) collective-permute-start(bf16[128,640]{1,0:T(8,128)(2,1)S(1)} %get-tuple-element.57), channel_id=1, source_target_pairs={{0,4},{4,0},{8,12},{12,8},{16,20},{20,16},{24,28},{28,24},{32,36},... | collective-permute-start | bytes 491528 | tf_op jit(solution)/shard_map/ppermute | solution.py:237
  (61 shorter events, 15.0 us)
Async XLA Ops:
  0.6 9.9 %copy-start = (bf16[1,1,256,640]{3,2,1,0:T(8,128)(2,1)S(1)}, bf16[1,1,256,640]{3,2,1,0:T(8,128)(2,1)}, u32[]{:S(2)}) copy-start(bf16[1,1,256,640]{3,2,1,0:T(8,128)(2,1)} %param.10) | copy-start | bytes 983044
  0.7 9.9 %copy-start.1 = (bf16[1,1,256,128]{3,2,1,0:T(8,128)(2,1)S(1)}, bf16[1,1,256,128]{3,2,1,0:T(8,128)(2,1)}, u32[]{:S(2)}) copy-start(bf16[1,1,256,128]{3,2,1,0:T(8,128)(2,1)} %param.11) | copy-start | bytes 196612
  0.7 9.9 %copy-start.4 = (bf16[1,32,128]{2,1,0:T(8,128)(2,1)S(1)}, bf16[1,32,128]{2,1,0:T(8,128)(2,1)}, u32[]{:S(2)}) copy-start(bf16[1,32,128]{2,1,0:T(8,128)(2,1)} %param.14) | copy-start | bytes 24580
  1.7 8.8 %copy-start.3 = (bf16[1,32,128]{2,1,0:T(8,128)(2,1)S(1)}, bf16[1,32,128]{2,1,0:T(8,128)(2,1)}, u32[]{:S(2)}) copy-start(bf16[1,32,128]{2,1,0:T(8,128)(2,1)} %param.13) | copy-start | bytes 24580
  1.8 9.8 %collective-permute-start = (bf16[128,640]{1,0:T(8,128)(2,1)S(1)}, bf16[128,640]{1,0:T(8,128)(2,1)S(1)}, u32[]{:S(2)}, u32[]{:S(2)}) collective-permute-start(bf16[128,640]{1,0:T(8,128)(2,1)S(1)} %get-tuple-element.79), channel_id=1, source_target_pairs={{0,4},{4,0},{8,12},{12,8},{16,20},{20,16},{24,28},{28,24},{32,36},... | collective-permute-start | bytes 491528 | tf_op jit(solution)/shard_map/ppermute | solution.py:237
  11.6 11.7 %collective-permute-start.1 = (bf16[2,128,640]{2,1,0:T(8,128)(2,1)S(1)}, bf16[2,128,640]{2,1,0:T(8,128)(2,1)S(1)}, u32[]{:S(2)}, u32[]{:S(2)}) collective-permute-start(bf16[2,128,640]{2,1,0:T(8,128)(2,1)S(1)} %pad_maximum_fusion.2), channel_id=1, source_target_pairs={{0,32},{4,20},{8,40},{12,28},{16,48},{20,4},{24,56},{28,12},{32,0}... | collective-permute-start | bytes 983048 | tf_op jit(solution)/shard_map/ppermute | solution.py:237
  23.4 23.7 %collective-permute-start.2 = (bf16[4,128,640]{2,1,0:T(8,128)(2,1)S(1)}, bf16[4,128,640]{2,1,0:T(8,128)(2,1)S(1)}, u32[]{:S(2)}, u32[]{:S(2)}) collective-permute-start(bf16[4,128,640]{2,1,0:T(8,128)(2,1)S(1)} %pad_maximum_fusion), channel_id=1, source_target_pairs={{0,8},{4,12},{8,0},{12,4},{16,24},{20,28},{24,16},{28,20},{32,40},... | collective-permute-start | bytes 1966088 | tf_op jit(solution)/shard_map/ppermute | solution.py:237
  27.3 39.6 %all-to-all-start.1 = ((bf16[16,32,256]{2,1,0:T(8,128)(2,1)}), bf16[16,32,256]{2,1,0:T(8,128)(2,1)S(1)}, u32[]{:S(2)}, u32[]{:S(2)}) async-start(bf16[16,32,256]{2,1,0:T(8,128)(2,1)} %get-tuple-element.43), calls=%async_computation.1 | async-start | bytes 524288 | tf_op jit(solution)/shard_map/all_to_all | solution.py:330
  47.1 9.4 %copy-start.8 = (f32[640]{0:T(1024)S(1)}, f32[640]{0:T(1024)}, u32[]{:S(2)}) copy-start(f32[640]{0:T(1024)} %param.15) | copy-start | bytes 7684
  47.1 19.7 %copy-start.2 = (bf16[1,1,256,128]{3,2,1,0:T(8,128)(2,1)S(1)}, bf16[1,1,256,128]{3,2,1,0:T(8,128)(2,1)}, u32[]{:S(2)}) copy-start(bf16[1,1,256,128]{3,2,1,0:T(8,128)(2,1)} %param.12) | copy-start | bytes 196612
  47.2 27.8 %collective-permute-start.3 = (bf16[2,128,640]{2,1,0:T(8,128)(2,1)S(1)}, bf16[2,128,640]{2,1,0:T(8,128)(2,1)S(1)}, u32[]{:S(2)}, u32[]{:S(2)}) collective-permute-start(bf16[2,128,640]{2,1,0:T(8,128)(2,1)S(1)} %pad_maximum_fusion.3), channel_id=1, source_target_pairs={{0,16},{4,36},{8,24},{12,44},{16,0},{20,52},{24,8},{28,60},{32,48}... | collective-permute-start | bytes 983048 | tf_op jit(solution)/shard_map/ppermute | solution.py:237
  71.1 4.0 %collective-permute-start.4 = (bf16[128,640]{1,0:T(8,128)(2,1)S(1)}, bf16[128,640]{1,0:T(8,128)(2,1)S(1)}, u32[]{:S(2)}, u32[]{:S(2)}) collective-permute-start(bf16[128,640]{1,0:T(8,128)(2,1)S(1)} %get-tuple-element.77), channel_id=1, source_target_pairs={{0,4},{4,0},{8,12},{12,8},{16,20},{20,16},{24,28},{28,24},{32,36},... | collective-permute-start | bytes 491528 | tf_op jit(solution)/shard_map/ppermute | solution.py:237
  75.1 15.8 %collective-permute-start.5 = (bf16[2,128,640]{2,1,0:T(8,128)(2,1)S(1)}, bf16[2,128,640]{2,1,0:T(8,128)(2,1)S(1)}, u32[]{:S(2)}, u32[]{:S(2)}) collective-permute-start(bf16[2,128,640]{2,1,0:T(8,128)(2,1)S(1)} %pad_maximum_fusion.4), channel_id=1, source_target_pairs={{0,32},{4,20},{8,40},{12,28},{16,48},{20,4},{24,56},{28,12},{32,0}... | collective-permute-start | bytes 983048 | tf_op jit(solution)/shard_map/ppermute | solution.py:237
  77.8 4.0 %collective-permute-start.6 = (bf16[128,640]{1,0:T(8,128)(2,1)S(1)}, bf16[128,640]{1,0:T(8,128)(2,1)S(1)}, u32[]{:S(2)}, u32[]{:S(2)}) collective-permute-start(bf16[128,640]{1,0:T(8,128)(2,1)S(1)} %get-tuple-element.50), channel_id=1, source_target_pairs={{0,4},{4,0},{8,12},{12,8},{16,20},{20,16},{24,28},{28,24},{32,36},... | collective-permute-start | bytes 491528 | tf_op jit(solution)/shard_map/ppermute | solution.py:237
  91.0 18.7 %collective-permute-start.7 = (bf16[4,128,640]{2,1,0:T(8,128)(2,1)S(1)}, bf16[4,128,640]{2,1,0:T(8,128)(2,1)S(1)}, u32[]{:S(2)}, u32[]{:S(2)}) collective-permute-start(bf16[4,128,640]{2,1,0:T(8,128)(2,1)S(1)} %pad_maximum_fusion.1), channel_id=1, source_target_pairs={{0,8},{4,12},{8,0},{12,4},{16,24},{20,28},{24,16},{28,20},{32,40},... | collective-permute-start | bytes 1966088 | tf_op jit(solution)/shard_map/ppermute | solution.py:237
  95.6 7.5 %collective-permute-start.9 = (bf16[8,40,256]{2,1,0:T(8,128)(2,1)S(1)}, bf16[8,40,256]{2,1,0:T(8,128)(2,1)S(1)}, u32[]{:S(2)}, u32[]{:S(2)}) collective-permute-start(bf16[8,40,256]{2,1,0:T(8,128)(2,1)S(1)} %fusion.6), channel_id=1, source_target_pairs={{0,4},{4,0},{8,12},{12,8},{16,20},{20,16},{24,28},{28,24},{32,36},... | collective-permute-start | bytes 491528 | tf_op jit(solution)/shard_map/ppermute | solution.py:237
  103.8 14.6 %all-to-all-start.2 = ((bf16[8,40,256]{2,1,0:T(8,128)(2,1)}), bf16[8,40,256]{2,1,0:T(8,128)(2,1)S(1)}, u32[]{:S(2)}, u32[]{:S(2)}) async-start(bf16[8,40,256]{2,1,0:T(8,128)(2,1)} %fusion.5), calls=%async_computation.2 | async-start | bytes 327680 | tf_op jit(solution)/shard_map/all_to_all | solution.py:397
  109.7 40.1 %collective-permute-start.8 = (bf16[2,128,640]{2,1,0:T(8,128)(2,1)S(1)}, bf16[2,128,640]{2,1,0:T(8,128)(2,1)S(1)}, u32[]{:S(2)}, u32[]{:S(2)}) collective-permute-start(bf16[2,128,640]{2,1,0:T(8,128)(2,1)S(1)} %pad_maximum_fusion.5), channel_id=1, source_target_pairs={{0,16},{4,36},{8,24},{12,44},{16,0},{20,52},{24,8},{28,60},{32,48}... | collective-permute-start | bytes 983048 | tf_op jit(solution)/shard_map/ppermute | solution.py:237
  119.0 30.7 %all-to-all-start.3 = ((f32[8,3,256]{2,1,0:T(4,128)}), f32[8,3,256]{2,1,0:T(4,128)S(1)}, u32[]{:S(2)}, u32[]{:S(2)}) async-start(f32[8,3,256]{2,1,0:T(4,128)} %broadcast_in_dim.45), calls=%async_computation.3 | async-start | bytes 65536 | tf_op jit(solution)/shard_map/all_to_all | solution.py:403
  136.0 10.8 %collective-permute-start.13 = (f32[8,128]{1,0:T(8,128)S(1)}, f32[8,128]{1,0:T(8,128)S(1)}, u32[]{:S(2)}, u32[]{:S(2)}) collective-permute-start(f32[8,128]{1,0:T(8,128)S(1)} %get-tuple-element.60.refs_0_), channel_id=1, source_target_pairs={{0,3},{1,0},{2,1},{3,2},{4,7},{5,4},{6,5},{7,6},{8,11},{9,8},{10,9... | collective-permute-start | bytes 12296 | tf_op jit(solution)/shard_map/ppermute | solution.py:384
  140.6 6.2 %collective-permute-start.12 = (f32[8,128]{1,0:T(8,128)S(1)}, f32[8,128]{1,0:T(8,128)S(1)}, u32[]{:S(2)}, u32[]{:S(2)}) collective-permute-start(f32[8,128]{1,0:T(8,128)S(1)} %get-tuple-element.60.refs_0_), channel_id=1, source_target_pairs={{0,2},{1,3},{2,0},{3,1},{4,6},{5,7},{6,4},{7,5},{8,10},{9,11},{10,... | collective-permute-start | bytes 12296 | tf_op jit(solution)/shard_map/ppermute | solution.py:384
  142.9 5.6 %collective-permute-start.11 = (f32[8,128]{1,0:T(8,128)S(1)}, f32[8,128]{1,0:T(8,128)S(1)}, u32[]{:S(2)}, u32[]{:S(2)}) collective-permute-start(f32[8,128]{1,0:T(8,128)S(1)} %get-tuple-element.60.refs_0_), channel_id=1, source_target_pairs={{0,1},{1,2},{2,3},{3,0},{4,5},{5,6},{6,7},{7,4},{8,9},{9,10},{10,1... | collective-permute-start | bytes 12296 | tf_op jit(solution)/shard_map/ppermute | solution.py:384
  149.8 15.1 %copy-start.7 = (f32[768]{0:T(1024)}, f32[768]{0:T(1024)S(1)}, u32[]{:S(2)}) copy-start(f32[768]{0:T(1024)S(1)} %reshape.144) | copy-start | bytes 9220
  149.9 15.5 %collective-permute-start.10 = (bf16[128,640]{1,0:T(8,128)(2,1)S(1)}, bf16[128,640]{1,0:T(8,128)(2,1)S(1)}, u32[]{:S(2)}, u32[]{:S(2)}) collective-permute-start(bf16[128,640]{1,0:T(8,128)(2,1)S(1)} %get-tuple-element.57), channel_id=1, source_target_pairs={{0,4},{4,0},{8,12},{12,8},{16,20},{20,16},{24,28},{28,24},{32,36},... | collective-permute-start | bytes 491528 | tf_op jit(solution)/shard_map/ppermute | solution.py:237
  (2 other events, 1.3 us)

commit v2 on v1

--- a/solution.py
+++ b/solution.py
@@ -196,15 +196,15 @@
         [gains, jnp.zeros((8 - GAIN_ROWS, 2 * HEAD), f32)], axis=0
     )
     tile = columns_to_tile([query_mix[:BLOCK], query_mix[BLOCK:], key_mix[:BLOCK], key_mix[BLOCK:]])
-    mix_ref[...] = tile
-
-
-def final_kernel(q_ref, k_ref, sums_ref, u_ref, w_ref, *refs):
-    *mix_refs, gq_ref, gk_ref = refs
+    for i in range(N_TENSOR):
+        mix_ref[i] = tile
+
+
+def final_kernel(q_ref, k_ref, sums_ref, u_ref, w_ref, mix_ref, gq_ref, gk_ref):
     query_factor, key_factor = factors(sums_ref)
-    total = mix_refs[0][...]
-    for mix_ref in mix_refs[1:]:
-        total = total + mix_ref[...]
+    total = mix_ref[0]
+    for i in range(1, N_TENSOR):
+        total = total + mix_ref[i]
     query_mix, key_mix = tile_to_columns(total)
     normed = q_ref[...].astype(f32) * query_factor
     gq_ref[...] = (
@@ -357,7 +357,7 @@
             ((RESP, HEAD), f32),
             ((RESP, HEAD), bf16),
             ((PROMPT, 2 * HEAD), f32),
-            ((8, BLOCK), f32),
+            ((N_TENSOR, 8, BLOCK), f32),
             ((8, 2 * HEAD), f32),
         ],
         [SMEM] + [VMEM] * 13,
@@ -380,8 +380,6 @@
     )
     out_four, gains, terms = lax.optimization_barrier((out_four, gains, terms))
     out_eight = to_ranks.eight(out_four)
-    turns = [[(i, (i + k) % N_TENSOR) for i in range(N_TENSOR)] for k in range(1, N_TENSOR)]
-    mix = [mix] + [lax.ppermute(mix, "tensor", turn) for turn in turns]
     owned = PROMPT // N_TRAINER
     terms = jnp.concatenate(
         [
@@ -394,7 +392,8 @@
         lax.dynamic_index_in_dim(terms, i, 1, keepdims=False) for i in (core, 1 - core)
     )
     terms = (near + swap(far.astype(bf16), 1, 1).astype(f32)).astype(bf16)
-    terms = lax.all_to_all(terms, "zlo", 0, 0, tiled=True)
+    mix = lax.all_to_all(mix, "tensor", 0, 0, tiled=True)
+    terms = lax.all_to_all(after(terms, mix), "zlo", 0, 0, tiled=True)
     terms = jnp.sum(terms.astype(f32), axis=0)
     gains = terms[owned : owned + GAIN_ROWS]
     terms = terms[:owned].astype(bf16)
@@ -419,7 +418,7 @@
     grad_queries, grad_keys = call(
         final_kernel,
         [((RESP, WIDTH), bf16), ((RESP, HEAD), bf16)],
-        [VMEM] * (5 + N_TENSOR),
+        [VMEM] * 6,
         [],
         0,
         query,
@@ -427,7 +426,7 @@
         sums,
         u,
         w,
-        *mix,
+        mix,
     )
     return (
         attn_out[None, None],

time: 167 us -> 169 us (1.012)
  the two profiles are of different devices: /device:TPU:1 before, /device:TPU:33 now
where the time goes in v2:
time: 169 us
  starting transfers between devices  94.3 us (56%)
  waiting for transfers between devices  37 us (22%)
  Pallas kernels  12.7 us (8%)
  blocking collectives  8.49 us (5%)
  between operations  6.93 us (4%)
  local copies, waits for them, and re-layouts  4.82 us (3%)
  other arithmetic  4.25 us (3%)
    ppermute x11, starting transfers between devices, swap(): return lax.ppermute(array, TRAINER, pairs)  51.3 us
    all_to_all x1, starting transfers between devices, on_device(): lax.all_to_all(pairs, TRAINER, 0, 0, tiled=True).reshape(PROMPT, 2 * HEAD)  18.5 us
    all_to_all x1, starting transfers between devices, on_device(): lax.all_to_all(jnp.broadcast_to(gains[None], (lax.axis_size(PROMPTS),) +...  17.2 us
    pallas_call x4, Pallas kernels, call(): pl.pallas_call(kernel, out_shape=[jax.ShapeDtypeStruct(s, d) for s, d in...  12.7 us
    ppermute x11, waiting for transfers between devices, swap(): return lax.ppermute(array, TRAINER, pairs)  12.2 us
    all_to_all x1, waiting for transfers between devices, on_device(): lax.all_to_all(jnp.broadcast_to(gains[None], (lax.axis_size(PROMPTS),) +...  11.5 us
    all_to_all x1, waiting for transfers between devices, on_device(): lax.all_to_all(pairs, TRAINER, 0, 0, tiled=True).reshape(PROMPT, 2 * HEAD)  9.77 us
    all_to_all x1, blocking collectives, on_device(): sums = lax.all_to_all(sums, 'tensor', 0, 0, tiled=True)  8.49 us
  transfers between devices with their start and end apart: 15, of which 8 were waited for; matrix products, arithmetic and copies ran while one was open for 3% of the time, Pallas kernels for 8%

profile of v2, /device:TPU:33, one launch (start us, length us, event | category | flops | bytes accessed | tf_op | source)
XLA Modules:
  0.0 168.5 jit_solution(15093339744588843591)
XLA Ops:
  1.8 2.6 %collective-permute-start = (bf16[128,640]{1,0:T(8,128)(2,1)S(1)}, bf16[128,640]{1,0:T(8,128)(2,1)S(1)}, u32[]{:S(2)}, u32[]{:S(2)}) collective-permute-start(bf16[128,640]{1,0:T(8,128)(2,1)S(1)} %get-tuple-element.81), channel_id=1, source_target_pairs={{0,4},{4,0},{8,12},{12,8},{16,20},{20,16},{24,28},{28,24},{32,36},... | collective-permute-start | bytes 491528 | tf_op jit(solution)/shard_map/ppermute | solution.py:237
  5.4 4.9 %collective-permute-start.1 = (bf16[2,128,640]{2,1,0:T(8,128)(2,1)S(1)}, bf16[2,128,640]{2,1,0:T(8,128)(2,1)S(1)}, u32[]{:S(2)}, u32[]{:S(2)}) collective-permute-start(bf16[2,128,640]{2,1,0:T(8,128)(2,1)S(1)} %pad_maximum_fusion.2), channel_id=1, source_target_pairs={{0,32},{4,20},{8,40},{12,28},{16,48},{20,4},{24,56},{28,12},{32,0}... | collective-permute-start | bytes 983048 | tf_op jit(solution)/shard_map/ppermute | solution.py:237
  10.3 8.5 %all_to_all.25.sums_ref = f32[4,8,128]{2,1,0:T(8,128)S(1)} all-to-all(f32[4,8,128]{2,1,0:T(8,128)S(1)} %get-tuple-element.40), channel_id=1, replica_groups=mesh['x'=4,'zhi'=2,'zlo'=8,'core'=2,'tensor'=4] {'tensor'}, dimensions={0} | all-to-all | bytes 32768 | tf_op jit(solution)/shard_map/all_to_all | solution.py:326
  18.8 4.0 %collective-permute-done.1 = bf16[2,128,640]{2,1,0:T(8,128)(2,1)S(1)} collective-permute-done((bf16[2,128,640]{2,1,0:T(8,128)(2,1)S(1)}, bf16[2,128,640]{2,1,0:T(8,128)(2,1)S(1)}, u32[]{:S(2)}, u32[]{:S(2)}) %collective-permute-start.1) | collective-permute-done | bytes 327712 | tf_op jit(solution)/shard_map/ppermute | solution.py:237
  22.9 1.9 %collective-permute-start.2 = (bf16[4,128,640]{2,1,0:T(8,128)(2,1)S(1)}, bf16[4,128,640]{2,1,0:T(8,128)(2,1)S(1)}, u32[]{:S(2)}, u32[]{:S(2)}) collective-permute-start(bf16[4,128,640]{2,1,0:T(8,128)(2,1)S(1)} %pad_maximum_fusion), channel_id=1, source_target_pairs={{0,8},{4,12},{8,0},{12,4},{16,24},{20,28},{24,16},{28,20},{32,40},... | collective-permute-start | bytes 1966088 | tf_op jit(solution)/shard_map/ppermute | solution.py:237
  24.8 18.5 %all-to-all-start.1 = ((bf16[16,32,256]{2,1,0:T(8,128)(2,1)}), bf16[16,32,256]{2,1,0:T(8,128)(2,1)S(1)}, u32[]{:S(2)}, u32[]{:S(2)}) async-start(bf16[16,32,256]{2,1,0:T(8,128)(2,1)} %get-tuple-element.44), calls=%async_computation.1 | async-start | bytes 524288 | tf_op jit(solution)/shard_map/all_to_all | solution.py:330
  46.1 7.1 %collective-permute-start.3 = (bf16[2,128,640]{2,1,0:T(8,128)(2,1)S(1)}, bf16[2,128,640]{2,1,0:T(8,128)(2,1)S(1)}, u32[]{:S(2)}, u32[]{:S(2)}) collective-permute-start(bf16[2,128,640]{2,1,0:T(8,128)(2,1)S(1)} %pad_maximum_fusion.3), channel_id=1, source_target_pairs={{0,16},{4,36},{8,24},{12,44},{16,0},{20,52},{24,8},{28,60},{32,48}... | collective-permute-start | bytes 983048 | tf_op jit(solution)/shard_map/ppermute | solution.py:237
  55.3 9.8 %all-to-all-done.1 = bf16[16,32,256]{2,1,0:T(8,128)(2,1)S(1)} async-done(((bf16[16,32,256]{2,1,0:T(8,128)(2,1)}), bf16[16,32,256]{2,1,0:T(8,128)(2,1)S(1)}, u32[]{:S(2)}, u32[]{:S(2)}) %all-to-all-start.1) | async-done | bytes 262176 | tf_op jit(solution)/shard_map/all_to_all | solution.py:330
  65.7 3.5 %shard_map.162 = (bf16[256,640]{1,0:T(8,128)(2,1)S(1)}, bf16[768,128]{1,0:T(8,128)(2,1)S(1)}, f32[8,256]{1,0:T(8,128)S(1)}, bf16[256,640]{1,0:T(8,128)(2,1)S(1)}) custom-call(s32[2]{0:T(128)S(1)} %pad_add_fusion.info_ref, bf16[256,640]{1,0:T(8,128)(2,1)S(1)} %bitcast.65, bf16[256,128]{1,0:T(8,128)(2,1)S(1)} %bitcast.74, bf16[256,128]{1,0:T(8,128)(2,1)S(1)} %bitcast.77, ...), custom_call_target="tpu_custom_call" | custom-call | tf_op jit(solution)/shard_map/pallas_call | solution.py:220
  69.2 1.9 %collective-permute-start.4 = (bf16[128,640]{1,0:T(8,128)(2,1)S(1)}, bf16[128,640]{1,0:T(8,128)(2,1)S(1)}, u32[]{:S(2)}, u32[]{:S(2)}) collective-permute-start(bf16[128,640]{1,0:T(8,128)(2,1)S(1)} %get-tuple-element.79), channel_id=1, source_target_pairs={{0,4},{4,0},{8,12},{12,8},{16,20},{20,16},{24,28},{28,24},{32,36},... | collective-permute-start | bytes 491528 | tf_op jit(solution)/shard_map/ppermute | solution.py:237
  71.2 3.0 %collective-permute-done.3 = bf16[2,128,640]{2,1,0:T(8,128)(2,1)S(1)} collective-permute-done((bf16[2,128,640]{2,1,0:T(8,128)(2,1)S(1)}, bf16[2,128,640]{2,1,0:T(8,128)(2,1)S(1)}, u32[]{:S(2)}, u32[]{:S(2)}) %collective-permute-start.3) | collective-permute-done | bytes 327712 | tf_op jit(solution)/shard_map/ppermute | solution.py:237
  74.3 2.5 %collective-permute-start.5 = (bf16[2,128,640]{2,1,0:T(8,128)(2,1)S(1)}, bf16[2,128,640]{2,1,0:T(8,128)(2,1)S(1)}, u32[]{:S(2)}, u32[]{:S(2)}) collective-permute-start(bf16[2,128,640]{2,1,0:T(8,128)(2,1)S(1)} %pad_maximum_fusion.4), channel_id=1, source_target_pairs={{0,32},{4,20},{8,40},{12,28},{16,48},{20,4},{24,56},{28,12},{32,0}... | collective-permute-start | bytes 983048 | tf_op jit(solution)/shard_map/ppermute | solution.py:237
  76.8 1.9 %collective-permute-start.6 = (bf16[128,640]{1,0:T(8,128)(2,1)S(1)}, bf16[128,640]{1,0:T(8,128)(2,1)S(1)}, u32[]{:S(2)}, u32[]{:S(2)}) collective-permute-start(bf16[128,640]{1,0:T(8,128)(2,1)S(1)} %get-tuple-element.51), channel_id=1, source_target_pairs={{0,4},{4,0},{8,12},{12,8},{16,20},{20,16},{24,28},{28,24},{32,36},... | collective-permute-start | bytes 491528 | tf_op jit(solution)/shard_map/ppermute | solution.py:237
  80.1 7.3 %shard_map.163 = (f32[256,640]{1,0:T(8,128)S(1)}, f32[256,128]{1,0:T(8,128)S(1)}, bf16[256,128]{1,0:T(8,128)(2,1)}, f32[512,256]{1,0:T(8,128)S(1)}, f32[4,8,128]{2,1,0:T(8,128)}, /*index=5*/f32[8,256]{1,0:T(8,128)S(1)}) custom-call(s32[2]{0:T(128)S(1)} %pad_add_fusion.info_ref, bf16[256,640]{1,0:T(8,128)(2,1)S(1)} %bitcast.66, ...), custom_call_target="tpu_custom_call" | custom-call | tf_op jit(solution)/shard_map/pallas_call | solution.py:220
  87.4 3.7 %collective-permute-done.5 = bf16[2,128,640]{2,1,0:T(8,128)(2,1)S(1)} collective-permute-done((bf16[2,128,640]{2,1,0:T(8,128)(2,1)S(1)}, bf16[2,128,640]{2,1,0:T(8,128)(2,1)S(1)}, u32[]{:S(2)}, u32[]{:S(2)}) %collective-permute-start.5) | collective-permute-done | bytes 327712 | tf_op jit(solution)/shard_map/ppermute | solution.py:237
  91.1 1.9 %collective-permute-start.7 = (bf16[4,128,640]{2,1,0:T(8,128)(2,1)S(1)}, bf16[4,128,640]{2,1,0:T(8,128)(2,1)S(1)}, u32[]{:S(2)}, u32[]{:S(2)}) collective-permute-start(bf16[4,128,640]{2,1,0:T(8,128)(2,1)S(1)} %pad_maximum_fusion.1), channel_id=1, source_target_pairs={{0,8},{4,12},{8,0},{12,4},{16,24},{20,28},{24,16},{28,20},{32,40},... | collective-permute-start | bytes 1966088 | tf_op jit(solution)/shard_map/ppermute | solution.py:237
  93.8 8.2 %collective-permute-start.9 = (bf16[8,40,256]{2,1,0:T(8,128)(2,1)}, bf16[8,40,256]{2,1,0:T(8,128)(2,1)S(1)}, u32[]{:S(2)}, u32[]{:S(2)}) collective-permute-start(bf16[8,40,256]{2,1,0:T(8,128)(2,1)} %fusion.6), channel_id=1, source_target_pairs={{0,4},{4,0},{8,12},{12,8},{16,20},{20,16},{24,28},{28,24},{32,36},... | collective-permute-start | bytes 491528 | tf_op jit(solution)/shard_map/ppermute | solution.py:237
  102.0 3.7 %all-to-all-start.2 = ((f32[4,8,128]{2,1,0:T(8,128)}), f32[4,8,128]{2,1,0:T(8,128)S(1)}, u32[]{:S(2)}, u32[]{:S(2)}) async-start(f32[4,8,128]{2,1,0:T(8,128)} %get-tuple-element.57), calls=%async_computation.2 | async-start | bytes 32768 | tf_op jit(solution)/shard_map/all_to_all | solution.py:395
  106.4 3.5 %all-to-all-done.2.mix_ref = f32[4,8,128]{2,1,0:T(8,128)S(1)} async-done(((f32[4,8,128]{2,1,0:T(8,128)}), f32[4,8,128]{2,1,0:T(8,128)S(1)}, u32[]{:S(2)}, u32[]{:S(2)}) %all-to-all-start.2) | async-done | bytes 16416 | tf_op jit(solution)/shard_map/all_to_all | solution.py:395
  109.9 3.6 %all-to-all-start.3 = ((bf16[8,40,256]{2,1,0:T(8,128)(2,1)}), bf16[8,40,256]{2,1,0:T(8,128)(2,1)S(1)}, u32[]{:S(2)}, u32[]{:S(2)}) async-start(bf16[8,40,256]{2,1,0:T(8,128)(2,1)} %fusion.5), calls=%async_computation.3 | async-start | bytes 327680 | tf_op jit(solution)/shard_map/all_to_all | solution.py:396
  116.4 7.0 %collective-permute-start.8 = (bf16[2,128,640]{2,1,0:T(8,128)(2,1)}, bf16[2,128,640]{2,1,0:T(8,128)(2,1)S(1)}, u32[]{:S(2)}, u32[]{:S(2)}) collective-permute-start(bf16[2,128,640]{2,1,0:T(8,128)(2,1)} %pad_maximum_fusion.5), channel_id=1, source_target_pairs={{0,16},{4,36},{8,24},{12,44},{16,0},{20,52},{24,8},{28,60},{32,48}... | collective-permute-start | bytes 983048 | tf_op jit(solution)/shard_map/ppermute | solution.py:237
  124.0 17.2 %all-to-all-start.4 = ((f32[8,3,256]{2,1,0:T(4,128)}), f32[8,3,256]{2,1,0:T(4,128)S(1)}, u32[]{:S(2)}, u32[]{:S(2)}) async-start(f32[8,3,256]{2,1,0:T(4,128)} %broadcast_in_dim.45), calls=%async_computation.4 | async-start | bytes 65536 | tf_op jit(solution)/shard_map/all_to_all | solution.py:402
  143.7 11.5 %all-to-all-done.4 = f32[8,3,256]{2,1,0:T(4,128)S(1)} async-done(((f32[8,3,256]{2,1,0:T(4,128)}), f32[8,3,256]{2,1,0:T(4,128)S(1)}, u32[]{:S(2)}, u32[]{:S(2)}) %all-to-all-start.4) | async-done | bytes 24608 | tf_op jit(solution)/shard_map/all_to_all | solution.py:402
  155.3 11.3 %collective-permute-start.10 = (bf16[128,640]{1,0:T(8,128)(2,1)S(1)}, bf16[128,640]{1,0:T(8,128)(2,1)S(1)}, u32[]{:S(2)}, u32[]{:S(2)}) collective-permute-start(bf16[128,640]{1,0:T(8,128)(2,1)S(1)} %get-tuple-element.60), channel_id=1, source_target_pairs={{0,4},{4,0},{8,12},{12,8},{16,20},{20,16},{24,28},{28,24},{32,36},... | collective-permute-start | bytes 491528 | tf_op jit(solution)/shard_map/ppermute | solution.py:237
  (57 shorter events, 12.5 us)
Async XLA Ops:
  0.6 3.7 %copy-start = (bf16[1,1,256,640]{3,2,1,0:T(8,128)(2,1)S(1)}, bf16[1,1,256,640]{3,2,1,0:T(8,128)(2,1)}, u32[]{:S(2)}) copy-start(bf16[1,1,256,640]{3,2,1,0:T(8,128)(2,1)} %param.10) | copy-start | bytes 983044
  0.7 3.7 %copy-start.1 = (bf16[1,1,256,128]{3,2,1,0:T(8,128)(2,1)S(1)}, bf16[1,1,256,128]{3,2,1,0:T(8,128)(2,1)}, u32[]{:S(2)}) copy-start(bf16[1,1,256,128]{3,2,1,0:T(8,128)(2,1)} %param.11) | copy-start | bytes 196612
  0.7 3.7 %copy-start.4 = (bf16[1,32,128]{2,1,0:T(8,128)(2,1)S(1)}, bf16[1,32,128]{2,1,0:T(8,128)(2,1)}, u32[]{:S(2)}) copy-start(bf16[1,32,128]{2,1,0:T(8,128)(2,1)} %param.14) | copy-start | bytes 24580
  1.7 2.6 %copy-start.3 = (bf16[1,32,128]{2,1,0:T(8,128)(2,1)S(1)}, bf16[1,32,128]{2,1,0:T(8,128)(2,1)}, u32[]{:S(2)}) copy-start(bf16[1,32,128]{2,1,0:T(8,128)(2,1)} %param.13) | copy-start | bytes 24580
  1.8 3.6 %collective-permute-start = (bf16[128,640]{1,0:T(8,128)(2,1)S(1)}, bf16[128,640]{1,0:T(8,128)(2,1)S(1)}, u32[]{:S(2)}, u32[]{:S(2)}) collective-permute-start(bf16[128,640]{1,0:T(8,128)(2,1)S(1)} %get-tuple-element.81), channel_id=1, source_target_pairs={{0,4},{4,0},{8,12},{12,8},{16,20},{20,16},{24,28},{28,24},{32,36},... | collective-permute-start | bytes 491528 | tf_op jit(solution)/shard_map/ppermute | solution.py:237
  5.4 17.4 %collective-permute-start.1 = (bf16[2,128,640]{2,1,0:T(8,128)(2,1)S(1)}, bf16[2,128,640]{2,1,0:T(8,128)(2,1)S(1)}, u32[]{:S(2)}, u32[]{:S(2)}) collective-permute-start(bf16[2,128,640]{2,1,0:T(8,128)(2,1)S(1)} %pad_maximum_fusion.2), channel_id=1, source_target_pairs={{0,32},{4,20},{8,40},{12,28},{16,48},{20,4},{24,56},{28,12},{32,0}... | collective-permute-start | bytes 983048 | tf_op jit(solution)/shard_map/ppermute | solution.py:237
  22.9 23.0 %collective-permute-start.2 = (bf16[4,128,640]{2,1,0:T(8,128)(2,1)S(1)}, bf16[4,128,640]{2,1,0:T(8,128)(2,1)S(1)}, u32[]{:S(2)}, u32[]{:S(2)}) collective-permute-start(bf16[4,128,640]{2,1,0:T(8,128)(2,1)S(1)} %pad_maximum_fusion), channel_id=1, source_target_pairs={{0,8},{4,12},{8,0},{12,4},{16,24},{20,28},{24,16},{28,20},{32,40},... | collective-permute-start | bytes 1966088 | tf_op jit(solution)/shard_map/ppermute | solution.py:237
  24.8 40.2 %all-to-all-start.1 = ((bf16[16,32,256]{2,1,0:T(8,128)(2,1)}), bf16[16,32,256]{2,1,0:T(8,128)(2,1)S(1)}, u32[]{:S(2)}, u32[]{:S(2)}) async-start(bf16[16,32,256]{2,1,0:T(8,128)(2,1)} %get-tuple-element.44), calls=%async_computation.1 | async-start | bytes 524288 | tf_op jit(solution)/shard_map/all_to_all | solution.py:330
  43.3 0.7 copy-start.6
  46.0 9.2 %copy-start.8 = (f32[640]{0:T(1024)S(1)}, f32[640]{0:T(1024)}, u32[]{:S(2)}) copy-start(f32[640]{0:T(1024)} %param.15) | copy-start | bytes 7684
  46.1 19.0 %copy-start.2 = (bf16[1,1,256,128]{3,2,1,0:T(8,128)(2,1)S(1)}, bf16[1,1,256,128]{3,2,1,0:T(8,128)(2,1)}, u32[]{:S(2)}) copy-start(bf16[1,1,256,128]{3,2,1,0:T(8,128)(2,1)} %param.12) | copy-start | bytes 196612
  46.1 28.1 %collective-permute-start.3 = (bf16[2,128,640]{2,1,0:T(8,128)(2,1)S(1)}, bf16[2,128,640]{2,1,0:T(8,128)(2,1)S(1)}, u32[]{:S(2)}, u32[]{:S(2)}) collective-permute-start(bf16[2,128,640]{2,1,0:T(8,128)(2,1)S(1)} %pad_maximum_fusion.3), channel_id=1, source_target_pairs={{0,16},{4,36},{8,24},{12,44},{16,0},{20,52},{24,8},{28,60},{32,48}... | collective-permute-start | bytes 983048 | tf_op jit(solution)/shard_map/ppermute | solution.py:237
  65.1 0.7 copy-start.5
  69.2 5.0 %collective-permute-start.4 = (bf16[128,640]{1,0:T(8,128)(2,1)S(1)}, bf16[128,640]{1,0:T(8,128)(2,1)S(1)}, u32[]{:S(2)}, u32[]{:S(2)}) collective-permute-start(bf16[128,640]{1,0:T(8,128)(2,1)S(1)} %get-tuple-element.79), channel_id=1, source_target_pairs={{0,4},{4,0},{8,12},{12,8},{16,20},{20,16},{24,28},{28,24},{32,36},... | collective-permute-start | bytes 491528 | tf_op jit(solution)/shard_map/ppermute | solution.py:237
  74.3 16.8 %collective-permute-start.5 = (bf16[2,128,640]{2,1,0:T(8,128)(2,1)S(1)}, bf16[2,128,640]{2,1,0:T(8,128)(2,1)S(1)}, u32[]{:S(2)}, u32[]{:S(2)}) collective-permute-start(bf16[2,128,640]{2,1,0:T(8,128)(2,1)S(1)} %pad_maximum_fusion.4), channel_id=1, source_target_pairs={{0,32},{4,20},{8,40},{12,28},{16,48},{20,4},{24,56},{28,12},{32,0}... | collective-permute-start | bytes 983048 | tf_op jit(solution)/shard_map/ppermute | solution.py:237
  76.8 3.3 %collective-permute-start.6 = (bf16[128,640]{1,0:T(8,128)(2,1)S(1)}, bf16[128,640]{1,0:T(8,128)(2,1)S(1)}, u32[]{:S(2)}, u32[]{:S(2)}) collective-permute-start(bf16[128,640]{1,0:T(8,128)(2,1)S(1)} %get-tuple-element.51), channel_id=1, source_target_pairs={{0,4},{4,0},{8,12},{12,8},{16,20},{20,16},{24,28},{28,24},{32,36},... | collective-permute-start | bytes 491528 | tf_op jit(solution)/shard_map/ppermute | solution.py:237
  91.1 24.4 %collective-permute-start.7 = (bf16[4,128,640]{2,1,0:T(8,128)(2,1)S(1)}, bf16[4,128,640]{2,1,0:T(8,128)(2,1)S(1)}, u32[]{:S(2)}, u32[]{:S(2)}) collective-permute-start(bf16[4,128,640]{2,1,0:T(8,128)(2,1)S(1)} %pad_maximum_fusion.1), channel_id=1, source_target_pairs={{0,8},{4,12},{8,0},{12,4},{16,24},{20,28},{24,16},{28,20},{32,40},... | collective-permute-start | bytes 1966088 | tf_op jit(solution)/shard_map/ppermute | solution.py:237
  93.8 12.0 %collective-permute-start.9 = (bf16[8,40,256]{2,1,0:T(8,128)(2,1)}, bf16[8,40,256]{2,1,0:T(8,128)(2,1)S(1)}, u32[]{:S(2)}, u32[]{:S(2)}) collective-permute-start(bf16[8,40,256]{2,1,0:T(8,128)(2,1)} %fusion.6), channel_id=1, source_target_pairs={{0,4},{4,0},{8,12},{12,8},{16,20},{20,16},{24,28},{28,24},{32,36},... | collective-permute-start | bytes 491528 | tf_op jit(solution)/shard_map/ppermute | solution.py:237
  102.0 8.0 %all-to-all-start.2 = ((f32[4,8,128]{2,1,0:T(8,128)}), f32[4,8,128]{2,1,0:T(8,128)S(1)}, u32[]{:S(2)}, u32[]{:S(2)}) async-start(f32[4,8,128]{2,1,0:T(8,128)} %get-tuple-element.57), calls=%async_computation.2 | async-start | bytes 32768 | tf_op jit(solution)/shard_map/all_to_all | solution.py:395
  109.9 13.4 %all-to-all-start.3 = ((bf16[8,40,256]{2,1,0:T(8,128)(2,1)}), bf16[8,40,256]{2,1,0:T(8,128)(2,1)S(1)}, u32[]{:S(2)}, u32[]{:S(2)}) async-start(bf16[8,40,256]{2,1,0:T(8,128)(2,1)} %fusion.5), calls=%async_computation.3 | async-start | bytes 327680 | tf_op jit(solution)/shard_map/all_to_all | solution.py:396
  116.4 38.9 %collective-permute-start.8 = (bf16[2,128,640]{2,1,0:T(8,128)(2,1)}, bf16[2,128,640]{2,1,0:T(8,128)(2,1)S(1)}, u32[]{:S(2)}, u32[]{:S(2)}) collective-permute-start(bf16[2,128,640]{2,1,0:T(8,128)(2,1)} %pad_maximum_fusion.5), channel_id=1, source_target_pairs={{0,16},{4,36},{8,24},{12,44},{16,0},{20,52},{24,8},{28,60},{32,48}... | collective-permute-start | bytes 983048 | tf_op jit(solution)/shard_map/ppermute | solution.py:237
  124.0 31.2 %all-to-all-start.4 = ((f32[8,3,256]{2,1,0:T(4,128)}), f32[8,3,256]{2,1,0:T(4,128)S(1)}, u32[]{:S(2)}, u32[]{:S(2)}) async-start(f32[8,3,256]{2,1,0:T(4,128)} %broadcast_in_dim.45), calls=%async_computation.4 | async-start | bytes 65536 | tf_op jit(solution)/shard_map/all_to_all | solution.py:402
  155.2 12.0 %copy-start.7 = (f32[768]{0:T(1024)}, f32[768]{0:T(1024)S(1)}, u32[]{:S(2)}) copy-start(f32[768]{0:T(1024)S(1)} %reshape.144) | copy-start | bytes 9220
  155.3 12.4 %collective-permute-start.10 = (bf16[128,640]{1,0:T(8,128)(2,1)S(1)}, bf16[128,640]{1,0:T(8,128)(2,1)S(1)}, u32[]{:S(2)}, u32[]{:S(2)}) collective-permute-start(bf16[128,640]{1,0:T(8,128)(2,1)S(1)} %get-tuple-element.60), channel_id=1, source_target_pairs={{0,4},{4,0},{8,12},{12,8},{16,20},{20,16},{24,28},{28,24},{32,36},... | collective-permute-start | bytes 491528 | tf_op jit(solution)/shard_map/ppermute | solution.py:237

commit v3 on v2

--- a/solution.py
+++ b/solution.py
@@ -93,16 +93,18 @@
 
 
 def forward_kernel(
-    info_ref, q_ref, k_ref, v_ref, kv_ref, sums_ref, qg_ref, kg_ref,
+    info_ref, q_ref, k_ref, v_ref, near_ref, far_ref, sums_ref, qg_ref, kg_ref,
     qn_ref, keys_ref, lse_ref, out_ref,
     values_t_ref, s_ref, p_ref,
 ):
     length = info_ref[0]
     query_factor, key_factor = factors(sums_ref)
     qn_ref[...] = (q_ref[...].astype(f32) * query_factor * qg_ref[...]).astype(bf16)
-    keys_ref[:PROMPT] = kv_ref[:, :HEAD]
+    keys_ref[:RESP] = near_ref[:, :HEAD]
+    keys_ref[RESP:PROMPT] = far_ref[:, :HEAD]
     keys_ref[PROMPT:] = (k_ref[...].astype(f32) * key_factor * kg_ref[...]).astype(bf16)
-    values_t_ref[:, :PROMPT] = kv_ref[:, HEAD:].astype(f32).T.astype(bf16)
+    values_t_ref[:, :RESP] = near_ref[:, HEAD:].astype(f32).T.astype(bf16)
+    values_t_ref[:, RESP:PROMPT] = far_ref[:, HEAD:].astype(f32).T.astype(bf16)
     values_t_ref[:, PROMPT:] = v_ref[...].astype(f32).T.astype(bf16)
     live = live_column(length)
     for h in range(GROUP):
@@ -132,9 +134,9 @@
 
 
 def backward_kernel(
-    info_ref, q_ref, k_ref, v_ref, kv_ref, sums_ref, qg_ref, kg_ref,
+    info_ref, q_ref, k_ref, v_ref, near_ref, far_ref, sums_ref, qg_ref, kg_ref,
     qn_ref, keys_ref, lse_ref, out_ref, own_ref, passed_ref,
-    u_ref, w_ref, gv_ref, terms_ref, mix_ref, gain_ref,
+    u_ref, w_ref, gv_ref, near_terms_ref, far_terms_ref, small_ref,
     keys_t_ref, grad_ref, ds_ref, dk_ref, dv_ref,
 ):
     length = info_ref[0]
@@ -157,10 +159,8 @@
         lse = lse_ref[h : h + 1]
         for c in range(CHUNKS):
             rows = slice(c * BLOCK, (c + 1) * BLOCK)
-            if c < PROMPT_CHUNKS:
-                value = kv_ref[rows, HEAD:]
-            else:
-                value = v_ref[(c - PROMPT_CHUNKS) * BLOCK : (c - PROMPT_CHUNKS + 1) * BLOCK]
+            part = slice(c % 2 * BLOCK, (c % 2 + 1) * BLOCK)
+            value = (near_ref[part, HEAD:], far_ref[part, HEAD:], v_ref[part])[c // 2]
             scores = masked(nt(keys_ref[rows], query) * SCALE, c, length)
             weights = jnp.exp(scores - lse)
             prob_grad = nt(value, grad)
@@ -180,8 +180,10 @@
         u_ref[:, cols] = u
         query_mix = query_mix + jnp.sum(u * normed, axis=1, keepdims=True)
         gain_rows.append(jnp.sum(grad_qn * normed, axis=0, keepdims=True))
-    terms_ref[:, :HEAD] = dk_ref[:PROMPT]
-    terms_ref[:, HEAD:] = dv_ref[:PROMPT]
+    near_terms_ref[:, :HEAD] = dk_ref[:RESP]
+    near_terms_ref[:, HEAD:] = dv_ref[:RESP]
+    far_terms_ref[:, :HEAD] = dk_ref[RESP:PROMPT].astype(bf16)
+    far_terms_ref[:, HEAD:] = dv_ref[RESP:PROMPT].astype(bf16)
     gv_ref[...] = dv_ref[PROMPT:].astype(bf16)
     grad_kn = dk_ref[PROMPT:]
     normed_key = k_ref[...].astype(f32) * key_factor
@@ -189,15 +191,9 @@
     w_ref[...] = w
     key_mix = jnp.sum(w * normed_key, axis=1, keepdims=True)
     gain_rows.append(jnp.sum(grad_kn * normed_key, axis=0, keepdims=True))
-    gains = jnp.concatenate(
-        [jnp.concatenate(gain_rows[i : i + 2], axis=1) for i in range(0, GROUP + 1, 2)], axis=0
-    )
-    gain_ref[...] = jnp.concatenate(
-        [gains, jnp.zeros((8 - GAIN_ROWS, 2 * HEAD), f32)], axis=0
-    )
     tile = columns_to_tile([query_mix[:BLOCK], query_mix[BLOCK:], key_mix[:BLOCK], key_mix[BLOCK:]])
-    for i in range(N_TENSOR):
-        mix_ref[i] = tile
+    gain_rows.append(jnp.zeros((8 - len(gain_rows), HEAD), f32))
+    small_ref[...] = jnp.concatenate([tile] + gain_rows, axis=0)
 
 
 def final_kernel(q_ref, k_ref, sums_ref, u_ref, w_ref, mix_ref, gq_ref, gk_ref):
@@ -327,16 +323,20 @@
     grad_four = to_home.four(grad_pair, sums)
     grad_four, pairs = lax.optimization_barrier((grad_four, pairs))
     grad_eight = to_home.eight(grad_four)
-    pairs = lax.all_to_all(pairs, TRAINER, 0, 0, tiled=True).reshape(PROMPT, 2 * HEAD)
+    pairs = lax.all_to_all(pairs, TRAINER, 0, 0, tiled=True)
     grad_wanted = to_home.wanted(grad_eight)
-    pairs = after(pairs, grad_wanted)
+    pairs = after(pairs, grad_wanted).reshape(N_TRAINER // 2, 2, -1, 2 * HEAD)
+    near, far = (
+        lax.dynamic_index_in_dim(pairs, i, 1, keepdims=False).reshape(RESP, 2 * HEAD)
+        for i in (core, 1 - core)
+    )
     grad_found = to_home.found(grad_eight, grad_wanted)
     info = jnp.stack([lengths[0, 0], core])
-    shared = (query, key, value, pairs, sums, q_row, k_row)
+    shared = (query, key, value, near, far, sums, q_row, k_row)
     query_n, key_list, lse, home_out = call(
         forward_kernel,
         [((RESP, WIDTH), bf16), ((KEYS, HEAD), bf16), ((8, RESP), f32), ((RESP, WIDTH), bf16)],
-        [SMEM] + [VMEM] * 7,
+        [SMEM] + [VMEM] * 8,
         [((HEAD, KEYS), bf16), ((KEYS, RESP), f32), ((KEYS, RESP), bf16)],
         0,
         info,
@@ -350,17 +350,17 @@
     grad_own = grad_found[0]
     grad_passed = to_home.passed(grad_found[1])
 
-    u, w, grad_values, terms, mix, gains = call(
+    u, w, grad_values, near_terms, far_terms, small = call(
         backward_kernel,
         [
             ((RESP, WIDTH), f32),
             ((RESP, HEAD), f32),
             ((RESP, HEAD), bf16),
-            ((PROMPT, 2 * HEAD), f32),
-            ((N_TENSOR, 8, BLOCK), f32),
-            ((8, 2 * HEAD), f32),
+            ((RESP, 2 * HEAD), f32),
+            ((RESP, 2 * HEAD), bf16),
+            ((16, HEAD), f32),
         ],
-        [SMEM] + [VMEM] * 13,
+        [SMEM] + [VMEM] * 14,
         [
             ((HEAD, KEYS), bf16),
             ((RESP, WIDTH), bf16),
@@ -378,33 +378,35 @@
         grad_own,
         grad_passed,
     )
-    out_four, gains, terms = lax.optimization_barrier((out_four, gains, terms))
+    out_four, small, far_terms = lax.optimization_barrier((out_four, small, far_terms))
     out_eight = to_ranks.eight(out_four)
+    passed_terms = swap(far_terms, 1, 1)
+    plane = ("x", "tensor")
+    small = lax.all_to_all(
+        jnp.broadcast_to(after(small, passed_terms)[None], (lax.axis_size(plane),) + small.shape), plane, 0, 0, tiled=True
+    ).reshape(-1, N_TENSOR, 16, HEAD)
+    mix = lax.dynamic_index_in_dim(small, lax.axis_index("x"), 0, keepdims=False)[:, :8]
+    gains = lax.dynamic_index_in_dim(small, lax.axis_index("tensor"), 1, keepdims=False)
+    gains = jnp.sum(gains[:, 8:], axis=0).reshape(-1, 2 * HEAD)
+    gains = jnp.concatenate([gains, jnp.zeros_like(gains)], axis=0)
     owned = PROMPT // N_TRAINER
+    terms = near_terms + passed_terms.astype(f32)
     terms = jnp.concatenate(
         [
-            terms.reshape(N_TRAINER, owned, 2 * HEAD),
-            jnp.broadcast_to(gains[None], (N_TRAINER,) + gains.shape),
+            terms.reshape(N_TRAINER // 2, owned, 2 * HEAD),
+            jnp.broadcast_to(gains[None], (N_TRAINER // 2,) + gains.shape),
         ],
         axis=1,
-    ).reshape(N_TRAINER // 2, 2, owned + gains.shape[0], 2 * HEAD)
-    near, far = (
-        lax.dynamic_index_in_dim(terms, i, 1, keepdims=False) for i in (core, 1 - core)
-    )
-    terms = (near + swap(far.astype(bf16), 1, 1).astype(f32)).astype(bf16)
-    mix = lax.all_to_all(mix, "tensor", 0, 0, tiled=True)
-    terms = lax.all_to_all(after(terms, mix), "zlo", 0, 0, tiled=True)
+    ).astype(bf16)
+    terms = lax.all_to_all(terms, "zlo", 0, 0, tiled=True)
     terms = jnp.sum(terms.astype(f32), axis=0)
     gains = terms[owned : owned + GAIN_ROWS]
     terms = terms[:owned].astype(bf16)
     out_wanted = to_ranks.wanted(out_eight)
     gains = after(gains, out_wanted)
+    ends = ("zhi", "core")
     gains = lax.all_to_all(
-        jnp.broadcast_to(gains[None], (lax.axis_size(PROMPTS),) + gains.shape),
-        PROMPTS,
-        0,
-        0,
-        tiled=True,
+        jnp.broadcast_to(gains[None], (lax.axis_size(ends),) + gains.shape), ends, 0, 0, tiled=True
     )
     gains = jnp.sum(gains, axis=0).reshape(-1)
     out_found = to_ranks.found(out_eight, out_wanted)

time: 169 us -> 173 us (1.024)
  the two profiles are of different devices: /device:TPU:33 before, /device:TPU:1 now
where the time goes in v3:
time: 173 us; the launch traced here: 172 us
  starting transfers between devices  98.1 us (57%)
  waiting for transfers between devices  38.3 us (22%)
  Pallas kernels  12.4 us (7%)
  between operations  6.93 us (4%)
  blocking collectives  6.56 us (4%)
  local copies, waits for them, and re-layouts  6.36 us (4%)
  other arithmetic  3.81 us (2%)
    ppermute x11, starting transfers between devices, swap(): return lax.ppermute(array, TRAINER, pairs)  43.6 us
    all_to_all x1, starting transfers between devices, on_device(): lax.all_to_all(jnp.broadcast_to(gains[None], (lax.axis_size(ends),) + gai...  23.7 us
    all_to_all x1, starting transfers between devices, on_device(): pairs = lax.all_to_all(pairs, TRAINER, 0, 0, tiled=True)  17.1 us
    ppermute x11, waiting for transfers between devices, swap(): return lax.ppermute(array, TRAINER, pairs)  15.4 us
    pallas_call x4, Pallas kernels, call(): pl.pallas_call(kernel, out_shape=[jax.ShapeDtypeStruct(s, d) for s, d in...  12.4 us
    all_to_all x1, waiting for transfers between devices, on_device(): lax.all_to_all(jnp.broadcast_to(gains[None], (lax.axis_size(ends),) + gai...  10.7 us
    all_to_all x1, starting transfers between devices, on_device(): terms = lax.all_to_all(terms, 'zlo', 0, 0, tiled=True)  7.37 us
    all_to_all x1, waiting for transfers between devices, on_device(): lax.all_to_all(jnp.broadcast_to(after(small, passed_terms)[None], (lax.ax...  6.68 us
  transfers between devices with their start and end apart: 15, of which 8 were waited for; matrix products, arithmetic and copies ran while one was open for 3% of the time, Pallas kernels for 7%

profile of v3, /device:TPU:1, one launch (start us, length us, event | category | flops | bytes accessed | tf_op | source)
XLA Modules:
  0.0 172.5 jit_solution(12710154096032794382)
XLA Ops:
  1.8 8.8 %collective-permute-start = (bf16[128,640]{1,0:T(8,128)(2,1)S(1)}, bf16[128,640]{1,0:T(8,128)(2,1)S(1)}, u32[]{:S(2)}, u32[]{:S(2)}) collective-permute-start(bf16[128,640]{1,0:T(8,128)(2,1)S(1)} %get-tuple-element.81), channel_id=1, source_target_pairs={{0,4},{4,0},{8,12},{12,8},{16,20},{20,16},{24,28},{28,24},{32,36},... | collective-permute-start | bytes 491528 | tf_op jit(solution)/shard_map/ppermute | solution.py:233
  11.6 1.9 %collective-permute-start.1 = (bf16[2,128,640]{2,1,0:T(8,128)(2,1)S(1)}, bf16[2,128,640]{2,1,0:T(8,128)(2,1)S(1)}, u32[]{:S(2)}, u32[]{:S(2)}) collective-permute-start(bf16[2,128,640]{2,1,0:T(8,128)(2,1)S(1)} %pad_maximum_fusion.2), channel_id=1, source_target_pairs={{0,32},{4,20},{8,40},{12,28},{16,48},{20,4},{24,56},{28,12},{32,0}... | collective-permute-start | bytes 983048 | tf_op jit(solution)/shard_map/ppermute | solution.py:233
  13.5 6.6 %all_to_all.25.sums_ref = f32[4,8,128]{2,1,0:T(8,128)S(1)} all-to-all(f32[4,8,128]{2,1,0:T(8,128)S(1)} %get-tuple-element.40), channel_id=1, replica_groups=mesh['x'=4,'zhi'=2,'zlo'=8,'core'=2,'tensor'=4] {'tensor'}, dimensions={0} | all-to-all | bytes 32768 | tf_op jit(solution)/shard_map/all_to_all | solution.py:322
  20.1 3.2 %collective-permute-done.1 = bf16[2,128,640]{2,1,0:T(8,128)(2,1)S(1)} collective-permute-done((bf16[2,128,640]{2,1,0:T(8,128)(2,1)S(1)}, bf16[2,128,640]{2,1,0:T(8,128)(2,1)S(1)}, u32[]{:S(2)}, u32[]{:S(2)}) %collective-permute-start.1) | collective-permute-done | bytes 327712 | tf_op jit(solution)/shard_map/ppermute | solution.py:233
  23.4 3.9 %collective-permute-start.2 = (bf16[4,128,640]{2,1,0:T(8,128)(2,1)S(1)}, bf16[4,128,640]{2,1,0:T(8,128)(2,1)S(1)}, u32[]{:S(2)}, u32[]{:S(2)}) collective-permute-start(bf16[4,128,640]{2,1,0:T(8,128)(2,1)S(1)} %pad_maximum_fusion), channel_id=1, source_target_pairs={{0,8},{4,12},{8,0},{12,4},{16,24},{20,28},{24,16},{28,20},{32,40},... | collective-permute-start | bytes 1966088 | tf_op jit(solution)/shard_map/ppermute | solution.py:233
  27.3 17.1 %all-to-all-start.1 = ((bf16[16,32,256]{2,1,0:T(8,128)(2,1)}), bf16[16,32,256]{2,1,0:T(8,128)(2,1)S(1)}, u32[]{:S(2)}, u32[]{:S(2)}) async-start(bf16[16,32,256]{2,1,0:T(8,128)(2,1)} %get-tuple-element.44), calls=%async_computation.1 | async-start | bytes 524288 | tf_op jit(solution)/shard_map/all_to_all | solution.py:326
  49.8 7.2 %collective-permute-start.3 = (bf16[2,128,640]{2,1,0:T(8,128)(2,1)S(1)}, bf16[2,128,640]{2,1,0:T(8,128)(2,1)S(1)}, u32[]{:S(2)}, u32[]{:S(2)}) collective-permute-start(bf16[2,128,640]{2,1,0:T(8,128)(2,1)S(1)} %pad_maximum_fusion.3), channel_id=1, source_target_pairs={{0,16},{4,36},{8,24},{12,44},{16,0},{20,52},{24,8},{28,60},{32,48}... | collective-permute-start | bytes 983048 | tf_op jit(solution)/shard_map/ppermute | solution.py:233
  57.1 5.5 %all-to-all-done.1 = bf16[16,32,256]{2,1,0:T(8,128)(2,1)S(1)} async-done(((bf16[16,32,256]{2,1,0:T(8,128)(2,1)}), bf16[16,32,256]{2,1,0:T(8,128)(2,1)S(1)}, u32[]{:S(2)}, u32[]{:S(2)}) %all-to-all-start.1) | async-done | bytes 262176 | tf_op jit(solution)/shard_map/all_to_all | solution.py:326
  63.4 3.5 %shard_map.162 = (bf16[256,640]{1,0:T(8,128)(2,1)S(1)}, bf16[768,128]{1,0:T(8,128)(2,1)S(1)}, f32[8,256]{1,0:T(8,128)S(1)}, bf16[256,640]{1,0:T(8,128)(2,1)S(1)}) custom-call(s32[2]{0:T(128)S(1)} %pad_add_fusion.info_ref, bf16[256,640]{1,0:T(8,128)(2,1)S(1)} %bitcast.68, bf16[256,128]{1,0:T(8,128)(2,1)S(1)} %bitcast.77, bf16[256,128]{1,0:T(8,128)(2,1)S(1)} %bitcast.80, ...), custom_call_target="tpu_custom_call" | custom-call | tf_op jit(solution)/shard_map/pallas_call | solution.py:216
  67.0 1.9 %collective-permute-start.4 = (bf16[128,640]{1,0:T(8,128)(2,1)S(1)}, bf16[128,640]{1,0:T(8,128)(2,1)S(1)}, u32[]{:S(2)}, u32[]{:S(2)}) collective-permute-start(bf16[128,640]{1,0:T(8,128)(2,1)S(1)} %get-tuple-element.79), channel_id=1, source_target_pairs={{0,4},{4,0},{8,12},{12,8},{16,20},{20,16},{24,28},{28,24},{32,36},... | collective-permute-start | bytes 491528 | tf_op jit(solution)/shard_map/ppermute | solution.py:233
  68.9 6.1 %collective-permute-done.3 = bf16[2,128,640]{2,1,0:T(8,128)(2,1)S(1)} collective-permute-done((bf16[2,128,640]{2,1,0:T(8,128)(2,1)S(1)}, bf16[2,128,640]{2,1,0:T(8,128)(2,1)S(1)}, u32[]{:S(2)}, u32[]{:S(2)}) %collective-permute-start.3) | collective-permute-done | bytes 327712 | tf_op jit(solution)/shard_map/ppermute | solution.py:233
  75.1 3.0 %collective-permute-start.5 = (bf16[2,128,640]{2,1,0:T(8,128)(2,1)S(1)}, bf16[2,128,640]{2,1,0:T(8,128)(2,1)S(1)}, u32[]{:S(2)}, u32[]{:S(2)}) collective-permute-start(bf16[2,128,640]{2,1,0:T(8,128)(2,1)S(1)} %pad_maximum_fusion.4), channel_id=1, source_target_pairs={{0,32},{4,20},{8,40},{12,28},{16,48},{20,4},{24,56},{28,12},{32,0}... | collective-permute-start | bytes 983048 | tf_op jit(solution)/shard_map/ppermute | solution.py:233
  78.1 2.5 %collective-permute-start.6 = (bf16[128,640]{1,0:T(8,128)(2,1)S(1)}, bf16[128,640]{1,0:T(8,128)(2,1)S(1)}, u32[]{:S(2)}, u32[]{:S(2)}) collective-permute-start(bf16[128,640]{1,0:T(8,128)(2,1)S(1)} %get-tuple-element.51), channel_id=1, source_target_pairs={{0,4},{4,0},{8,12},{12,8},{16,20},{20,16},{24,28},{28,24},{32,36},... | collective-permute-start | bytes 491528 | tf_op jit(solution)/shard_map/ppermute | solution.py:233
  81.6 7.0 %shard_map.163 = (f32[256,640]{1,0:T(8,128)S(1)}, f32[256,128]{1,0:T(8,128)S(1)}, bf16[256,128]{1,0:T(8,128)(2,1)}, f32[256,256]{1,0:T(8,128)S(1)}, bf16[256,256]{1,0:T(8,128)(2,1)S(1)}, /*index=5*/f32[16,128]{1,0:T(8,128)S(1)}) custom-call(s32[2]{0:T(128)S(1)} %pad_add_fusion.info_ref, bf16[256,640]{1,0:T(8,128)(2,1)S(1)} %bitcast.69, ...), custom_call_target="tpu_custom_call" | custom-call | tf_op jit(solution)/shard_map/pallas_call | solution.py:216
  88.6 5.0 %collective-permute-done.5 = bf16[2,128,640]{2,1,0:T(8,128)(2,1)S(1)} collective-permute-done((bf16[2,128,640]{2,1,0:T(8,128)(2,1)S(1)}, bf16[2,128,640]{2,1,0:T(8,128)(2,1)S(1)}, u32[]{:S(2)}, u32[]{:S(2)}) %collective-permute-start.5) | collective-permute-done | bytes 327712 | tf_op jit(solution)/shard_map/ppermute | solution.py:233
  93.7 1.9 %collective-permute-start.9 = (bf16[256,256]{1,0:T(8,128)(2,1)S(1)}, bf16[256,256]{1,0:T(8,128)(2,1)S(1)}, u32[]{:S(2)}, u32[]{:S(2)}) collective-permute-start(bf16[256,256]{1,0:T(8,128)(2,1)S(1)} %get-tuple-element.56), channel_id=1, source_target_pairs={{0,4},{4,0},{8,12},{12,8},{16,20},{20,16},{24,28},{28,24},{32,36},... | collective-permute-start | bytes 393224 | tf_op jit(solution)/shard_map/ppermute | solution.py:233
  95.6 2.5 %collective-permute-start.7 = (bf16[4,128,640]{2,1,0:T(8,128)(2,1)S(1)}, bf16[4,128,640]{2,1,0:T(8,128)(2,1)S(1)}, u32[]{:S(2)}, u32[]{:S(2)}) collective-permute-start(bf16[4,128,640]{2,1,0:T(8,128)(2,1)S(1)} %pad_maximum_fusion.1), channel_id=1, source_target_pairs={{0,8},{4,12},{8,0},{12,4},{16,24},{20,28},{24,16},{28,20},{32,40},... | collective-permute-start | bytes 1966088 | tf_op jit(solution)/shard_map/ppermute | solution.py:233
  98.8 6.3 %all-to-all-start.2 = ((f32[16,16,128]{2,1,0:T(8,128)}), f32[16,16,128]{2,1,0:T(8,128)S(1)}, u32[]{:S(2)}, u32[]{:S(2)}) async-start(f32[16,16,128]{2,1,0:T(8,128)} %broadcast_in_dim.51), calls=%async_computation.2 | async-start | bytes 262144 | tf_op jit(solution)/shard_map/all_to_all | solution.py:385
  105.1 6.7 %all-to-all-done.2 = f32[16,16,128]{2,1,0:T(8,128)S(1)} async-done(((f32[16,16,128]{2,1,0:T(8,128)}), f32[16,16,128]{2,1,0:T(8,128)S(1)}, u32[]{:S(2)}, u32[]{:S(2)}) %all-to-all-start.2) | async-done | bytes 131104 | tf_op jit(solution)/shard_map/all_to_all | solution.py:385
  112.5 7.4 %all-to-all-start.3 = ((bf16[8,40,256]{2,1,0:T(8,128)(2,1)}), bf16[8,40,256]{2,1,0:T(8,128)(2,1)S(1)}, u32[]{:S(2)}, u32[]{:S(2)}) async-start(bf16[8,40,256]{2,1,0:T(8,128)(2,1)} %pad_maximum_fusion.6), calls=%async_computation.3 | async-start | bytes 327680 | tf_op jit(solution)/shard_map/all_to_all | solution.py:401
  122.0 7.3 %collective-permute-start.8 = (bf16[2,128,640]{2,1,0:T(8,128)(2,1)S(1)}, bf16[2,128,640]{2,1,0:T(8,128)(2,1)}, u32[]{:S(2)}, u32[]{:S(2)}) collective-permute-start(bf16[2,128,640]{2,1,0:T(8,128)(2,1)S(1)} %pad_maximum_fusion.5), channel_id=1, source_target_pairs={{0,16},{4,36},{8,24},{12,44},{16,0},{20,52},{24,8},{28,60},{32,48}... | collective-permute-start | bytes 983048 | tf_op jit(solution)/shard_map/ppermute | solution.py:233
  131.3 23.7 %all-to-all-start.4 = ((f32[4,3,256]{2,1,0:T(4,128)}), f32[4,3,256]{2,1,0:T(4,128)S(1)}, u32[]{:S(2)}, u32[]{:S(2)}) async-start(f32[4,3,256]{2,1,0:T(4,128)} %broadcast_in_dim.53), calls=%async_computation.4 | async-start | bytes 32768 | tf_op jit(solution)/shard_map/all_to_all | solution.py:408
  156.1 10.7 %all-to-all-done.4 = f32[4,3,256]{2,1,0:T(4,128)S(1)} async-done(((f32[4,3,256]{2,1,0:T(4,128)}), f32[4,3,256]{2,1,0:T(4,128)S(1)}, u32[]{:S(2)}, u32[]{:S(2)}) %all-to-all-start.4) | async-done | bytes 12320 | tf_op jit(solution)/shard_map/all_to_all | solution.py:408
  167.9 2.6 %collective-permute-start.10 = (bf16[128,640]{1,0:T(8,128)(2,1)S(1)}, bf16[128,640]{1,0:T(8,128)(2,1)S(1)}, u32[]{:S(2)}, u32[]{:S(2)}) collective-permute-start(bf16[128,640]{1,0:T(8,128)(2,1)S(1)} %get-tuple-element.60), channel_id=1, source_target_pairs={{0,4},{4,0},{8,12},{12,8},{16,20},{20,16},{24,28},{28,24},{32,36},... | collective-permute-start | bytes 491528 | tf_op jit(solution)/shard_map/ppermute | solution.py:233
  (65 shorter events, 13.3 us)
Async XLA Ops:
  0.6 9.9 %copy-start = (bf16[1,1,256,640]{3,2,1,0:T(8,128)(2,1)S(1)}, bf16[1,1,256,640]{3,2,1,0:T(8,128)(2,1)}, u32[]{:S(2)}) copy-start(bf16[1,1,256,640]{3,2,1,0:T(8,128)(2,1)} %param.10) | copy-start | bytes 983044
  0.7 9.9 %copy-start.1 = (bf16[1,1,256,128]{3,2,1,0:T(8,128)(2,1)S(1)}, bf16[1,1,256,128]{3,2,1,0:T(8,128)(2,1)}, u32[]{:S(2)}) copy-start(bf16[1,1,256,128]{3,2,1,0:T(8,128)(2,1)} %param.11) | copy-start | bytes 196612
  0.7 9.9 %copy-start.4 = (bf16[1,32,128]{2,1,0:T(8,128)(2,1)S(1)}, bf16[1,32,128]{2,1,0:T(8,128)(2,1)}, u32[]{:S(2)}) copy-start(bf16[1,32,128]{2,1,0:T(8,128)(2,1)} %param.14) | copy-start | bytes 24580
  1.8 8.8 %copy-start.3 = (bf16[1,32,128]{2,1,0:T(8,128)(2,1)S(1)}, bf16[1,32,128]{2,1,0:T(8,128)(2,1)}, u32[]{:S(2)}) copy-start(bf16[1,32,128]{2,1,0:T(8,128)(2,1)} %param.13) | copy-start | bytes 24580
  1.8 9.8 %collective-permute-start = (bf16[128,640]{1,0:T(8,128)(2,1)S(1)}, bf16[128,640]{1,0:T(8,128)(2,1)S(1)}, u32[]{:S(2)}, u32[]{:S(2)}) collective-permute-start(bf16[128,640]{1,0:T(8,128)(2,1)S(1)} %get-tuple-element.81), channel_id=1, source_target_pairs={{0,4},{4,0},{8,12},{12,8},{16,20},{20,16},{24,28},{28,24},{32,36},... | collective-permute-start | bytes 491528 | tf_op jit(solution)/shard_map/ppermute | solution.py:233
  11.6 11.7 %collective-permute-start.1 = (bf16[2,128,640]{2,1,0:T(8,128)(2,1)S(1)}, bf16[2,128,640]{2,1,0:T(8,128)(2,1)S(1)}, u32[]{:S(2)}, u32[]{:S(2)}) collective-permute-start(bf16[2,128,640]{2,1,0:T(8,128)(2,1)S(1)} %pad_maximum_fusion.2), channel_id=1, source_target_pairs={{0,32},{4,20},{8,40},{12,28},{16,48},{20,4},{24,56},{28,12},{32,0}... | collective-permute-start | bytes 983048 | tf_op jit(solution)/shard_map/ppermute | solution.py:233
  23.4 26.3 %collective-permute-start.2 = (bf16[4,128,640]{2,1,0:T(8,128)(2,1)S(1)}, bf16[4,128,640]{2,1,0:T(8,128)(2,1)S(1)}, u32[]{:S(2)}, u32[]{:S(2)}) collective-permute-start(bf16[4,128,640]{2,1,0:T(8,128)(2,1)S(1)} %pad_maximum_fusion), channel_id=1, source_target_pairs={{0,8},{4,12},{8,0},{12,4},{16,24},{20,28},{24,16},{28,20},{32,40},... | collective-permute-start | bytes 1966088 | tf_op jit(solution)/shard_map/ppermute | solution.py:233
  27.3 35.3 %all-to-all-start.1 = ((bf16[16,32,256]{2,1,0:T(8,128)(2,1)}), bf16[16,32,256]{2,1,0:T(8,128)(2,1)S(1)}, u32[]{:S(2)}, u32[]{:S(2)}) async-start(bf16[16,32,256]{2,1,0:T(8,128)(2,1)} %get-tuple-element.44), calls=%async_computation.1 | async-start | bytes 524288 | tf_op jit(solution)/shard_map/all_to_all | solution.py:326
  44.4 0.7 copy-start.6
  49.0 0.7 copy-start.8
  49.8 25.2 %collective-permute-start.3 = (bf16[2,128,640]{2,1,0:T(8,128)(2,1)S(1)}, bf16[2,128,640]{2,1,0:T(8,128)(2,1)S(1)}, u32[]{:S(2)}, u32[]{:S(2)}) collective-permute-start(bf16[2,128,640]{2,1,0:T(8,128)(2,1)S(1)} %pad_maximum_fusion.3), channel_id=1, source_target_pairs={{0,16},{4,36},{8,24},{12,44},{16,0},{20,52},{24,8},{28,60},{32,48}... | collective-permute-start | bytes 983048 | tf_op jit(solution)/shard_map/ppermute | solution.py:233
  62.6 0.8 copy-start.2
  62.6 0.8 copy-start.5
  67.0 8.1 %collective-permute-start.4 = (bf16[128,640]{1,0:T(8,128)(2,1)S(1)}, bf16[128,640]{1,0:T(8,128)(2,1)S(1)}, u32[]{:S(2)}, u32[]{:S(2)}) collective-permute-start(bf16[128,640]{1,0:T(8,128)(2,1)S(1)} %get-tuple-element.79), channel_id=1, source_target_pairs={{0,4},{4,0},{8,12},{12,8},{16,20},{20,16},{24,28},{28,24},{32,36},... | collective-permute-start | bytes 491528 | tf_op jit(solution)/shard_map/ppermute | solution.py:233
  75.1 18.5 %collective-permute-start.5 = (bf16[2,128,640]{2,1,0:T(8,128)(2,1)S(1)}, bf16[2,128,640]{2,1,0:T(8,128)(2,1)S(1)}, u32[]{:S(2)}, u32[]{:S(2)}) collective-permute-start(bf16[2,128,640]{2,1,0:T(8,128)(2,1)S(1)} %pad_maximum_fusion.4), channel_id=1, source_target_pairs={{0,32},{4,20},{8,40},{12,28},{16,48},{20,4},{24,56},{28,12},{32,0}... | collective-permute-start | bytes 983048 | tf_op jit(solution)/shard_map/ppermute | solution.py:233
  78.1 3.5 %collective-permute-start.6 = (bf16[128,640]{1,0:T(8,128)(2,1)S(1)}, bf16[128,640]{1,0:T(8,128)(2,1)S(1)}, u32[]{:S(2)}, u32[]{:S(2)}) collective-permute-start(bf16[128,640]{1,0:T(8,128)(2,1)S(1)} %get-tuple-element.51), channel_id=1, source_target_pairs={{0,4},{4,0},{8,12},{12,8},{16,20},{20,16},{24,28},{28,24},{32,36},... | collective-permute-start | bytes 491528 | tf_op jit(solution)/shard_map/ppermute | solution.py:233
  93.7 4.4 %collective-permute-start.9 = (bf16[256,256]{1,0:T(8,128)(2,1)S(1)}, bf16[256,256]{1,0:T(8,128)(2,1)S(1)}, u32[]{:S(2)}, u32[]{:S(2)}) collective-permute-start(bf16[256,256]{1,0:T(8,128)(2,1)S(1)} %get-tuple-element.56), channel_id=1, source_target_pairs={{0,4},{4,0},{8,12},{12,8},{16,20},{20,16},{24,28},{28,24},{32,36},... | collective-permute-start | bytes 393224 | tf_op jit(solution)/shard_map/ppermute | solution.py:233
  95.6 26.3 %collective-permute-start.7 = (bf16[4,128,640]{2,1,0:T(8,128)(2,1)S(1)}, bf16[4,128,640]{2,1,0:T(8,128)(2,1)S(1)}, u32[]{:S(2)}, u32[]{:S(2)}) collective-permute-start(bf16[4,128,640]{2,1,0:T(8,128)(2,1)S(1)} %pad_maximum_fusion.1), channel_id=1, source_target_pairs={{0,8},{4,12},{8,0},{12,4},{16,24},{20,28},{24,16},{28,20},{32,40},... | collective-permute-start | bytes 1966088 | tf_op jit(solution)/shard_map/ppermute | solution.py:233
  98.8 13.0 %all-to-all-start.2 = ((f32[16,16,128]{2,1,0:T(8,128)}), f32[16,16,128]{2,1,0:T(8,128)S(1)}, u32[]{:S(2)}, u32[]{:S(2)}) async-start(f32[16,16,128]{2,1,0:T(8,128)} %broadcast_in_dim.51), calls=%async_computation.2 | async-start | bytes 262144 | tf_op jit(solution)/shard_map/all_to_all | solution.py:385
  112.5 18.1 %all-to-all-start.3 = ((bf16[8,40,256]{2,1,0:T(8,128)(2,1)}), bf16[8,40,256]{2,1,0:T(8,128)(2,1)S(1)}, u32[]{:S(2)}, u32[]{:S(2)}) async-start(bf16[8,40,256]{2,1,0:T(8,128)(2,1)} %pad_maximum_fusion.6), calls=%async_computation.3 | async-start | bytes 327680 | tf_op jit(solution)/shard_map/all_to_all | solution.py:401
  122.0 44.8 %collective-permute-start.8 = (bf16[2,128,640]{2,1,0:T(8,128)(2,1)S(1)}, bf16[2,128,640]{2,1,0:T(8,128)(2,1)}, u32[]{:S(2)}, u32[]{:S(2)}) collective-permute-start(bf16[2,128,640]{2,1,0:T(8,128)(2,1)S(1)} %pad_maximum_fusion.5), channel_id=1, source_target_pairs={{0,16},{4,36},{8,24},{12,44},{16,0},{20,52},{24,8},{28,60},{32,48}... | collective-permute-start | bytes 983048 | tf_op jit(solution)/shard_map/ppermute | solution.py:233
  131.3 35.5 %all-to-all-start.4 = ((f32[4,3,256]{2,1,0:T(4,128)}), f32[4,3,256]{2,1,0:T(4,128)S(1)}, u32[]{:S(2)}, u32[]{:S(2)}) async-start(f32[4,3,256]{2,1,0:T(4,128)} %broadcast_in_dim.53), calls=%async_computation.4 | async-start | bytes 32768 | tf_op jit(solution)/shard_map/all_to_all | solution.py:408
  166.8 4.3 %copy-start.7 = (f32[768]{0:T(1024)}, f32[768]{0:T(1024)S(1)}, u32[]{:S(2)}) copy-start(f32[768]{0:T(1024)S(1)} %reshape.162) | copy-start | bytes 9220
  167.9 3.8 %collective-permute-start.10 = (bf16[128,640]{1,0:T(8,128)(2,1)S(1)}, bf16[128,640]{1,0:T(8,128)(2,1)S(1)}, u32[]{:S(2)}, u32[]{:S(2)}) collective-permute-start(bf16[128,640]{1,0:T(8,128)(2,1)S(1)} %get-tuple-element.60), channel_id=1, source_target_pairs={{0,4},{4,0},{8,12},{12,8},{16,20},{20,16},{24,28},{28,24},{32,36},... | collective-permute-start | bytes 491528 | tf_op jit(solution)/shard_map/ppermute | solution.py:233

commit v4 on v2

--- a/solution.py
+++ b/solution.py
@@ -409,7 +409,7 @@
     gains = jnp.sum(gains, axis=0).reshape(-1)
     out_found = to_ranks.found(out_eight, out_wanted)
 
-    out_own, out_passed = out_found[0], to_ranks.passed(after(out_found[1], gains))
+    out_own, out_passed = out_found[0], after(to_ranks.passed(out_found[1]), gains)
     attn_out = jnp.where(
         core == 0,
         jnp.concatenate([out_own, out_passed], axis=0),

time: 169 us -> 166 us (0.982)
  the two profiles are of different devices: /device:TPU:33 before, /device:TPU:32 now
where the time goes in v4:
time: 166 us; the launch traced here: 165 us
  starting transfers between devices  80.7 us (49%)
  waiting for transfers between devices  46.3 us (28%)
  Pallas kernels  12.7 us (8%)
  blocking collectives  9.63 us (6%)
  between operations  6.92 us (4%)
  local copies, waits for them, and re-layouts  4.82 us (3%)
  other arithmetic  4.25 us (3%)
    ppermute x11, starting transfers between devices, swap(): return lax.ppermute(array, TRAINER, pairs)  46.4 us
    all_to_all x1, starting transfers between devices, on_device(): lax.all_to_all(jnp.broadcast_to(gains[None], (lax.axis_size(PROMPTS),) +...  17.5 us
    pallas_call x4, Pallas kernels, call(): pl.pallas_call(kernel, out_shape=[jax.ShapeDtypeStruct(s, d) for s, d in...  12.7 us
    all_to_all x1, waiting for transfers between devices, on_device(): lax.all_to_all(jnp.broadcast_to(gains[None], (lax.axis_size(PROMPTS),) +...  12.4 us
    all_to_all x1, waiting for transfers between devices, on_device(): lax.all_to_all(pairs, TRAINER, 0, 0, tiled=True).reshape(PROMPT, 2 * HEAD)  11.9 us
    ppermute x11, waiting for transfers between devices, swap(): return lax.ppermute(array, TRAINER, pairs)  10.9 us
    all_to_all x1, blocking collectives, on_device(): sums = lax.all_to_all(sums, 'tensor', 0, 0, tiled=True)  9.63 us
    all_to_all x1, starting transfers between devices, on_device(): lax.all_to_all(pairs, TRAINER, 0, 0, tiled=True).reshape(PROMPT, 2 * HEAD)  8.65 us
  transfers between devices with their start and end apart: 15, of which 9 were waited for; matrix products, arithmetic and copies ran while one was open for 3% of the time, Pallas kernels for 8%

profile of v4, /device:TPU:32, one launch (start us, length us, event | category | flops | bytes accessed | tf_op | source)
XLA Modules:
  0.0 165.3 jit_solution(16914627053923847828)
XLA Ops:
  1.8 1.9 %collective-permute-start = (bf16[128,640]{1,0:T(8,128)(2,1)S(1)}, bf16[128,640]{1,0:T(8,128)(2,1)S(1)}, u32[]{:S(2)}, u32[]{:S(2)}) collective-permute-start(bf16[128,640]{1,0:T(8,128)(2,1)S(1)} %get-tuple-element.81), channel_id=1, source_target_pairs={{0,4},{4,0},{8,12},{12,8},{16,20},{20,16},{24,28},{28,24},{32,36},... | collective-permute-start | bytes 491528 | tf_op jit(solution)/shard_map/ppermute | solution.py:237
  5.1 9.1 %collective-permute-start.1 = (bf16[2,128,640]{2,1,0:T(8,128)(2,1)S(1)}, bf16[2,128,640]{2,1,0:T(8,128)(2,1)S(1)}, u32[]{:S(2)}, u32[]{:S(2)}) collective-permute-start(bf16[2,128,640]{2,1,0:T(8,128)(2,1)S(1)} %pad_maximum_fusion.2), channel_id=1, source_target_pairs={{0,32},{4,20},{8,40},{12,28},{16,48},{20,4},{24,56},{28,12},{32,0}... | collective-permute-start | bytes 983048 | tf_op jit(solution)/shard_map/ppermute | solution.py:237
  14.2 9.6 %all_to_all.25.sums_ref = f32[4,8,128]{2,1,0:T(8,128)S(1)} all-to-all(f32[4,8,128]{2,1,0:T(8,128)S(1)} %get-tuple-element.40), channel_id=1, replica_groups=mesh['x'=4,'zhi'=2,'zlo'=8,'core'=2,'tensor'=4] {'tensor'}, dimensions={0} | all-to-all | bytes 32768 | tf_op jit(solution)/shard_map/all_to_all | solution.py:326
  24.7 9.6 %collective-permute-start.2 = (bf16[4,128,640]{2,1,0:T(8,128)(2,1)S(1)}, bf16[4,128,640]{2,1,0:T(8,128)(2,1)S(1)}, u32[]{:S(2)}, u32[]{:S(2)}) collective-permute-start(bf16[4,128,640]{2,1,0:T(8,128)(2,1)S(1)} %pad_maximum_fusion), channel_id=1, source_target_pairs={{0,8},{4,12},{8,0},{12,4},{16,24},{20,28},{24,16},{28,20},{32,40},... | collective-permute-start | bytes 1966088 | tf_op jit(solution)/shard_map/ppermute | solution.py:237
  34.4 8.7 %all-to-all-start.1 = ((bf16[16,32,256]{2,1,0:T(8,128)(2,1)}), bf16[16,32,256]{2,1,0:T(8,128)(2,1)S(1)}, u32[]{:S(2)}, u32[]{:S(2)}) async-start(bf16[16,32,256]{2,1,0:T(8,128)(2,1)} %get-tuple-element.44), calls=%async_computation.1 | async-start | bytes 524288 | tf_op jit(solution)/shard_map/all_to_all | solution.py:330
  45.8 4.4 %collective-permute-start.3 = (bf16[2,128,640]{2,1,0:T(8,128)(2,1)S(1)}, bf16[2,128,640]{2,1,0:T(8,128)(2,1)S(1)}, u32[]{:S(2)}, u32[]{:S(2)}) collective-permute-start(bf16[2,128,640]{2,1,0:T(8,128)(2,1)S(1)} %pad_maximum_fusion.3), channel_id=1, source_target_pairs={{0,16},{4,36},{8,24},{12,44},{16,0},{20,52},{24,8},{28,60},{32,48}... | collective-permute-start | bytes 983048 | tf_op jit(solution)/shard_map/ppermute | solution.py:237
  52.2 11.9 %all-to-all-done.1 = bf16[16,32,256]{2,1,0:T(8,128)(2,1)S(1)} async-done(((bf16[16,32,256]{2,1,0:T(8,128)(2,1)}), bf16[16,32,256]{2,1,0:T(8,128)(2,1)S(1)}, u32[]{:S(2)}, u32[]{:S(2)}) %all-to-all-start.1) | async-done | bytes 262176 | tf_op jit(solution)/shard_map/all_to_all | solution.py:330
  64.8 3.5 %shard_map.162 = (bf16[256,640]{1,0:T(8,128)(2,1)S(1)}, bf16[768,128]{1,0:T(8,128)(2,1)S(1)}, f32[8,256]{1,0:T(8,128)S(1)}, bf16[256,640]{1,0:T(8,128)(2,1)S(1)}) custom-call(s32[2]{0:T(128)S(1)} %pad_add_fusion.info_ref, bf16[256,640]{1,0:T(8,128)(2,1)S(1)} %bitcast.65, bf16[256,128]{1,0:T(8,128)(2,1)S(1)} %bitcast.74, bf16[256,128]{1,0:T(8,128)(2,1)S(1)} %bitcast.77, ...), custom_call_target="tpu_custom_call" | custom-call | tf_op jit(solution)/shard_map/pallas_call | solution.py:220
  68.3 2.6 %collective-permute-start.4 = (bf16[128,640]{1,0:T(8,128)(2,1)S(1)}, bf16[128,640]{1,0:T(8,128)(2,1)S(1)}, u32[]{:S(2)}, u32[]{:S(2)}) collective-permute-start(bf16[128,640]{1,0:T(8,128)(2,1)S(1)} %get-tuple-element.79), channel_id=1, source_target_pairs={{0,4},{4,0},{8,12},{12,8},{16,20},{20,16},{24,28},{28,24},{32,36},... | collective-permute-start | bytes 491528 | tf_op jit(solution)/shard_map/ppermute | solution.py:237
  72.0 3.9 %collective-permute-start.5 = (bf16[2,128,640]{2,1,0:T(8,128)(2,1)S(1)}, bf16[2,128,640]{2,1,0:T(8,128)(2,1)S(1)}, u32[]{:S(2)}, u32[]{:S(2)}) collective-permute-start(bf16[2,128,640]{2,1,0:T(8,128)(2,1)S(1)} %pad_maximum_fusion.4), channel_id=1, source_target_pairs={{0,32},{4,20},{8,40},{12,28},{16,48},{20,4},{24,56},{28,12},{32,0}... | collective-permute-start | bytes 983048 | tf_op jit(solution)/shard_map/ppermute | solution.py:237
  75.9 2.7 %collective-permute-start.6 = (bf16[128,640]{1,0:T(8,128)(2,1)S(1)}, bf16[128,640]{1,0:T(8,128)(2,1)S(1)}, u32[]{:S(2)}, u32[]{:S(2)}) collective-permute-start(bf16[128,640]{1,0:T(8,128)(2,1)S(1)} %get-tuple-element.51), channel_id=1, source_target_pairs={{0,4},{4,0},{8,12},{12,8},{16,20},{20,16},{24,28},{28,24},{32,36},... | collective-permute-start | bytes 491528 | tf_op jit(solution)/shard_map/ppermute | solution.py:237
  79.6 7.3 %shard_map.163 = (f32[256,640]{1,0:T(8,128)S(1)}, f32[256,128]{1,0:T(8,128)S(1)}, bf16[256,128]{1,0:T(8,128)(2,1)}, f32[512,256]{1,0:T(8,128)S(1)}, f32[4,8,128]{2,1,0:T(8,128)}, /*index=5*/f32[8,256]{1,0:T(8,128)S(1)}) custom-call(s32[2]{0:T(128)S(1)} %pad_add_fusion.info_ref, bf16[256,640]{1,0:T(8,128)(2,1)S(1)} %bitcast.66, ...), custom_call_target="tpu_custom_call" | custom-call | tf_op jit(solution)/shard_map/pallas_call | solution.py:220
  86.9 7.7 %collective-permute-done.5 = bf16[2,128,640]{2,1,0:T(8,128)(2,1)S(1)} collective-permute-done((bf16[2,128,640]{2,1,0:T(8,128)(2,1)S(1)}, bf16[2,128,640]{2,1,0:T(8,128)(2,1)S(1)}, u32[]{:S(2)}, u32[]{:S(2)}) %collective-permute-start.5) | collective-permute-done | bytes 327712 | tf_op jit(solution)/shard_map/ppermute | solution.py:237
  94.6 4.1 %collective-permute-start.7 = (bf16[4,128,640]{2,1,0:T(8,128)(2,1)S(1)}, bf16[4,128,640]{2,1,0:T(8,128)(2,1)S(1)}, u32[]{:S(2)}, u32[]{:S(2)}) collective-permute-start(bf16[4,128,640]{2,1,0:T(8,128)(2,1)S(1)} %pad_maximum_fusion.1), channel_id=1, source_target_pairs={{0,8},{4,12},{8,0},{12,4},{16,24},{20,28},{24,16},{28,20},{32,40},... | collective-permute-start | bytes 1966088 | tf_op jit(solution)/shard_map/ppermute | solution.py:237
  99.4 1.9 %collective-permute-start.10 = (bf16[8,40,256]{2,1,0:T(8,128)(2,1)}, bf16[8,40,256]{2,1,0:T(8,128)(2,1)S(1)}, u32[]{:S(2)}, u32[]{:S(2)}) collective-permute-start(bf16[8,40,256]{2,1,0:T(8,128)(2,1)} %fusion.6), channel_id=1, source_target_pairs={{0,4},{4,0},{8,12},{12,8},{16,20},{20,16},{24,28},{28,24},{32,36},... | collective-permute-start | bytes 491528 | tf_op jit(solution)/shard_map/ppermute | solution.py:237
  101.3 4.0 %all-to-all-start.2 = ((f32[4,8,128]{2,1,0:T(8,128)}), f32[4,8,128]{2,1,0:T(8,128)S(1)}, u32[]{:S(2)}, u32[]{:S(2)}) async-start(f32[4,8,128]{2,1,0:T(8,128)} %get-tuple-element.57), calls=%async_computation.2 | async-start | bytes 32768 | tf_op jit(solution)/shard_map/all_to_all | solution.py:395
  106.0 4.7 %all-to-all-done.2.mix_ref = f32[4,8,128]{2,1,0:T(8,128)S(1)} async-done(((f32[4,8,128]{2,1,0:T(8,128)}), f32[4,8,128]{2,1,0:T(8,128)S(1)}, u32[]{:S(2)}, u32[]{:S(2)}) %all-to-all-start.2) | async-done | bytes 16416 | tf_op jit(solution)/shard_map/all_to_all | solution.py:395
  110.7 4.2 %all-to-all-start.3 = ((bf16[8,40,256]{2,1,0:T(8,128)(2,1)}), bf16[8,40,256]{2,1,0:T(8,128)(2,1)S(1)}, u32[]{:S(2)}, u32[]{:S(2)}) async-start(bf16[8,40,256]{2,1,0:T(8,128)(2,1)} %fusion.5), calls=%async_computation.3 | async-start | bytes 327680 | tf_op jit(solution)/shard_map/all_to_all | solution.py:396
  117.7 4.3 %collective-permute-start.8 = (bf16[2,128,640]{2,1,0:T(8,128)(2,1)}, bf16[2,128,640]{2,1,0:T(8,128)(2,1)S(1)}, u32[]{:S(2)}, u32[]{:S(2)}) collective-permute-start(bf16[2,128,640]{2,1,0:T(8,128)(2,1)} %pad_maximum_fusion.5), channel_id=1, source_target_pairs={{0,16},{4,36},{8,24},{12,44},{16,0},{20,52},{24,8},{28,60},{32,48}... | collective-permute-start | bytes 983048 | tf_op jit(solution)/shard_map/ppermute | solution.py:237
  123.3 1.1 shard_map.164
  124.4 6.4 %all-to-all-done.3 = bf16[8,40,256]{2,1,0:T(8,128)(2,1)S(1)} async-done(((bf16[8,40,256]{2,1,0:T(8,128)(2,1)}), bf16[8,40,256]{2,1,0:T(8,128)(2,1)S(1)}, u32[]{:S(2)}, u32[]{:S(2)}) %all-to-all-start.3) | async-done | bytes 163872 | tf_op jit(solution)/shard_map/all_to_all | solution.py:396
  131.4 17.5 %all-to-all-start.4 = ((f32[8,3,256]{2,1,0:T(4,128)}), f32[8,3,256]{2,1,0:T(4,128)S(1)}, u32[]{:S(2)}, u32[]{:S(2)}) async-start(f32[8,3,256]{2,1,0:T(4,128)} %broadcast_in_dim.45), calls=%async_computation.4 | async-start | bytes 65536 | tf_op jit(solution)/shard_map/all_to_all | solution.py:402
  149.0 1.9 %collective-permute-start.9 = (bf16[128,640]{1,0:T(8,128)(2,1)S(1)}, bf16[128,640]{1,0:T(8,128)(2,1)S(1)}, u32[]{:S(2)}, u32[]{:S(2)}) collective-permute-start(bf16[128,640]{1,0:T(8,128)(2,1)S(1)} %get-tuple-element.71), channel_id=1, source_target_pairs={{0,4},{4,0},{8,12},{12,8},{16,20},{20,16},{24,28},{28,24},{32,36},... | collective-permute-start | bytes 491528 | tf_op jit(solution)/shard_map/ppermute | solution.py:237
  151.6 12.4 %all-to-all-done.4 = f32[8,3,256]{2,1,0:T(4,128)S(1)} async-done(((f32[8,3,256]{2,1,0:T(4,128)}), f32[8,3,256]{2,1,0:T(4,128)S(1)}, u32[]{:S(2)}, u32[]{:S(2)}) %all-to-all-start.4) | async-done | bytes 24608 | tf_op jit(solution)/shard_map/all_to_all | solution.py:402
  (57 shorter events, 13.1 us)
Async XLA Ops:
  0.6 3.0 %copy-start = (bf16[1,1,256,640]{3,2,1,0:T(8,128)(2,1)S(1)}, bf16[1,1,256,640]{3,2,1,0:T(8,128)(2,1)}, u32[]{:S(2)}) copy-start(bf16[1,1,256,640]{3,2,1,0:T(8,128)(2,1)} %param.10) | copy-start | bytes 983044
  0.7 3.0 %copy-start.1 = (bf16[1,1,256,128]{3,2,1,0:T(8,128)(2,1)S(1)}, bf16[1,1,256,128]{3,2,1,0:T(8,128)(2,1)}, u32[]{:S(2)}) copy-start(bf16[1,1,256,128]{3,2,1,0:T(8,128)(2,1)} %param.11) | copy-start | bytes 196612
  0.7 3.0 %copy-start.4 = (bf16[1,32,128]{2,1,0:T(8,128)(2,1)S(1)}, bf16[1,32,128]{2,1,0:T(8,128)(2,1)}, u32[]{:S(2)}) copy-start(bf16[1,32,128]{2,1,0:T(8,128)(2,1)} %param.14) | copy-start | bytes 24580
  1.7 2.0 %copy-start.3 = (bf16[1,32,128]{2,1,0:T(8,128)(2,1)S(1)}, bf16[1,32,128]{2,1,0:T(8,128)(2,1)}, u32[]{:S(2)}) copy-start(bf16[1,32,128]{2,1,0:T(8,128)(2,1)} %param.13) | copy-start | bytes 24580
  1.8 3.3 %collective-permute-start = (bf16[128,640]{1,0:T(8,128)(2,1)S(1)}, bf16[128,640]{1,0:T(8,128)(2,1)S(1)}, u32[]{:S(2)}, u32[]{:S(2)}) collective-permute-start(bf16[128,640]{1,0:T(8,128)(2,1)S(1)} %get-tuple-element.81), channel_id=1, source_target_pairs={{0,4},{4,0},{8,12},{12,8},{16,20},{20,16},{24,28},{28,24},{32,36},... | collective-permute-start | bytes 491528 | tf_op jit(solution)/shard_map/ppermute | solution.py:237
  5.1 19.6 %collective-permute-start.1 = (bf16[2,128,640]{2,1,0:T(8,128)(2,1)S(1)}, bf16[2,128,640]{2,1,0:T(8,128)(2,1)S(1)}, u32[]{:S(2)}, u32[]{:S(2)}) collective-permute-start(bf16[2,128,640]{2,1,0:T(8,128)(2,1)S(1)} %pad_maximum_fusion.2), channel_id=1, source_target_pairs={{0,32},{4,20},{8,40},{12,28},{16,48},{20,4},{24,56},{28,12},{32,0}... | collective-permute-start | bytes 983048 | tf_op jit(solution)/shard_map/ppermute | solution.py:237
  24.7 20.9 %collective-permute-start.2 = (bf16[4,128,640]{2,1,0:T(8,128)(2,1)S(1)}, bf16[4,128,640]{2,1,0:T(8,128)(2,1)S(1)}, u32[]{:S(2)}, u32[]{:S(2)}) collective-permute-start(bf16[4,128,640]{2,1,0:T(8,128)(2,1)S(1)} %pad_maximum_fusion), channel_id=1, source_target_pairs={{0,8},{4,12},{8,0},{12,4},{16,24},{20,28},{24,16},{28,20},{32,40},... | collective-permute-start | bytes 1966088 | tf_op jit(solution)/shard_map/ppermute | solution.py:237
  34.4 29.8 %all-to-all-start.1 = ((bf16[16,32,256]{2,1,0:T(8,128)(2,1)}), bf16[16,32,256]{2,1,0:T(8,128)(2,1)S(1)}, u32[]{:S(2)}, u32[]{:S(2)}) async-start(bf16[16,32,256]{2,1,0:T(8,128)(2,1)} %get-tuple-element.44), calls=%async_computation.1 | async-start | bytes 524288 | tf_op jit(solution)/shard_map/all_to_all | solution.py:330
  43.0 0.7 copy-start.6
  45.7 6.5 %copy-start.8 = (f32[640]{0:T(1024)S(1)}, f32[640]{0:T(1024)}, u32[]{:S(2)}) copy-start(f32[640]{0:T(1024)} %param.15) | copy-start | bytes 7684
  45.7 18.4 %copy-start.2 = (bf16[1,1,256,128]{3,2,1,0:T(8,128)(2,1)S(1)}, bf16[1,1,256,128]{3,2,1,0:T(8,128)(2,1)}, u32[]{:S(2)}) copy-start(bf16[1,1,256,128]{3,2,1,0:T(8,128)(2,1)} %param.12) | copy-start | bytes 196612
  45.8 25.2 %collective-permute-start.3 = (bf16[2,128,640]{2,1,0:T(8,128)(2,1)S(1)}, bf16[2,128,640]{2,1,0:T(8,128)(2,1)S(1)}, u32[]{:S(2)}, u32[]{:S(2)}) collective-permute-start(bf16[2,128,640]{2,1,0:T(8,128)(2,1)S(1)} %pad_maximum_fusion.3), channel_id=1, source_target_pairs={{0,16},{4,36},{8,24},{12,44},{16,0},{20,52},{24,8},{28,60},{32,48}... | collective-permute-start | bytes 983048 | tf_op jit(solution)/shard_map/ppermute | solution.py:237
  64.2 0.7 copy-start.5
  68.3 3.6 %collective-permute-start.4 = (bf16[128,640]{1,0:T(8,128)(2,1)S(1)}, bf16[128,640]{1,0:T(8,128)(2,1)S(1)}, u32[]{:S(2)}, u32[]{:S(2)}) collective-permute-start(bf16[128,640]{1,0:T(8,128)(2,1)S(1)} %get-tuple-element.79), channel_id=1, source_target_pairs={{0,4},{4,0},{8,12},{12,8},{16,20},{20,16},{24,28},{28,24},{32,36},... | collective-permute-start | bytes 491528 | tf_op jit(solution)/shard_map/ppermute | solution.py:237
  72.0 22.5 %collective-permute-start.5 = (bf16[2,128,640]{2,1,0:T(8,128)(2,1)S(1)}, bf16[2,128,640]{2,1,0:T(8,128)(2,1)S(1)}, u32[]{:S(2)}, u32[]{:S(2)}) collective-permute-start(bf16[2,128,640]{2,1,0:T(8,128)(2,1)S(1)} %pad_maximum_fusion.4), channel_id=1, source_target_pairs={{0,32},{4,20},{8,40},{12,28},{16,48},{20,4},{24,56},{28,12},{32,0}... | collective-permute-start | bytes 983048 | tf_op jit(solution)/shard_map/ppermute | solution.py:237
  75.9 3.7 %collective-permute-start.6 = (bf16[128,640]{1,0:T(8,128)(2,1)S(1)}, bf16[128,640]{1,0:T(8,128)(2,1)S(1)}, u32[]{:S(2)}, u32[]{:S(2)}) collective-permute-start(bf16[128,640]{1,0:T(8,128)(2,1)S(1)} %get-tuple-element.51), channel_id=1, source_target_pairs={{0,4},{4,0},{8,12},{12,8},{16,20},{20,16},{24,28},{28,24},{32,36},... | collective-permute-start | bytes 491528 | tf_op jit(solution)/shard_map/ppermute | solution.py:237
  94.6 22.2 %collective-permute-start.7 = (bf16[4,128,640]{2,1,0:T(8,128)(2,1)S(1)}, bf16[4,128,640]{2,1,0:T(8,128)(2,1)S(1)}, u32[]{:S(2)}, u32[]{:S(2)}) collective-permute-start(bf16[4,128,640]{2,1,0:T(8,128)(2,1)S(1)} %pad_maximum_fusion.1), channel_id=1, source_target_pairs={{0,8},{4,12},{8,0},{12,4},{16,24},{20,28},{24,16},{28,20},{32,40},... | collective-permute-start | bytes 1966088 | tf_op jit(solution)/shard_map/ppermute | solution.py:237
  99.4 5.9 %collective-permute-start.10 = (bf16[8,40,256]{2,1,0:T(8,128)(2,1)}, bf16[8,40,256]{2,1,0:T(8,128)(2,1)S(1)}, u32[]{:S(2)}, u32[]{:S(2)}) collective-permute-start(bf16[8,40,256]{2,1,0:T(8,128)(2,1)} %fusion.6), channel_id=1, source_target_pairs={{0,4},{4,0},{8,12},{12,8},{16,20},{20,16},{24,28},{28,24},{32,36},... | collective-permute-start | bytes 491528 | tf_op jit(solution)/shard_map/ppermute | solution.py:237
  101.3 9.4 %all-to-all-start.2 = ((f32[4,8,128]{2,1,0:T(8,128)}), f32[4,8,128]{2,1,0:T(8,128)S(1)}, u32[]{:S(2)}, u32[]{:S(2)}) async-start(f32[4,8,128]{2,1,0:T(8,128)} %get-tuple-element.57), calls=%async_computation.2 | async-start | bytes 32768 | tf_op jit(solution)/shard_map/all_to_all | solution.py:395
  110.7 20.1 %all-to-all-start.3 = ((bf16[8,40,256]{2,1,0:T(8,128)(2,1)}), bf16[8,40,256]{2,1,0:T(8,128)(2,1)S(1)}, u32[]{:S(2)}, u32[]{:S(2)}) async-start(bf16[8,40,256]{2,1,0:T(8,128)(2,1)} %fusion.5), calls=%async_computation.3 | async-start | bytes 327680 | tf_op jit(solution)/shard_map/all_to_all | solution.py:396
  117.7 31.3 %collective-permute-start.8 = (bf16[2,128,640]{2,1,0:T(8,128)(2,1)}, bf16[2,128,640]{2,1,0:T(8,128)(2,1)S(1)}, u32[]{:S(2)}, u32[]{:S(2)}) collective-permute-start(bf16[2,128,640]{2,1,0:T(8,128)(2,1)} %pad_maximum_fusion.5), channel_id=1, source_target_pairs={{0,16},{4,36},{8,24},{12,44},{16,0},{20,52},{24,8},{28,60},{32,48}... | collective-permute-start | bytes 983048 | tf_op jit(solution)/shard_map/ppermute | solution.py:237
  131.4 32.5 %all-to-all-start.4 = ((f32[8,3,256]{2,1,0:T(4,128)}), f32[8,3,256]{2,1,0:T(4,128)S(1)}, u32[]{:S(2)}, u32[]{:S(2)}) async-start(f32[8,3,256]{2,1,0:T(4,128)} %broadcast_in_dim.45), calls=%async_computation.4 | async-start | bytes 65536 | tf_op jit(solution)/shard_map/all_to_all | solution.py:402
  149.0 15.4 %collective-permute-start.9 = (bf16[128,640]{1,0:T(8,128)(2,1)S(1)}, bf16[128,640]{1,0:T(8,128)(2,1)S(1)}, u32[]{:S(2)}, u32[]{:S(2)}) collective-permute-start(bf16[128,640]{1,0:T(8,128)(2,1)S(1)} %get-tuple-element.71), channel_id=1, source_target_pairs={{0,4},{4,0},{8,12},{12,8},{16,20},{20,16},{24,28},{28,24},{32,36},... | collective-permute-start | bytes 491528 | tf_op jit(solution)/shard_map/ppermute | solution.py:237
  163.9 1.3 copy-start.7
